TPU v7x, 32 devices: a whole 2x2x4 slice. The times are simulated.
32 devices in a mesh: pts: 8 (over z, y), blk: 4 (over x, core).
Axes of the slice: x: 2, y: 2, z: 4, core: 2. Of those that a mesh axis runs over, the one named last changes fastest.
Arguments:
- points: bfloat16 [16384, 512], P('pts', 'blk'), may hold values from -6 to 6
- neighbours: int32 [16384, 27], P('pts'), may hold values from 0 to 16383, as said below
- patch_ids: int32 [16384], P('pts'), may hold values from 0 to 31, as said below
- conv_weight: bfloat16 [27, 512, 512], P(None, 'blk'), may hold values from -0.0546875 to 0.0546875
- conv_bias: float32 [512], P('blk'), may hold values from -3 to 3
- cpe_weight: bfloat16 [512, 512], P('blk'), may hold values from -0.25 to 0.25
- cpe_bias: float32 [512], P('blk'), may hold values from -3 to 3
- cpe_gain: float32 [512], P('blk'), may hold values from 0.1 to 1.9
- cpe_shift: float32 [512], P('blk'), may hold values from -1.75 to 1.75
- first_gain: float32 [512], P('blk'), may hold values from 0.1 to 1.9
- first_shift: float32 [512], P('blk'), may hold values from -1.75 to 1.75
- qkv_weight: bfloat16 [512, 3, 512], P(None, None, 'blk'), may hold values from -0.25 to 0.25
- query_value_bias: float32 [2, 512], P(None, 'blk'), may hold values from -3 to 3
- proj_weight: bfloat16 [512, 512], P('blk'), may hold values from -4 to 4
- proj_bias: float32 [512], P('blk'), may hold values from -3 to 3
- second_gain: float32 [512], P('blk'), may hold values from 0.1 to 1.9
- second_shift: float32 [512], P('blk'), may hold values from -1.75 to 1.75
- hidden_weight: bfloat16 [512, 2048], P(None, 'blk'), may hold values from -0.25 to 0.25
- hidden_bias: float32 [2048], P('blk'), may hold values from -3 to 3
- output_weight: bfloat16 [2048, 512], P('blk'), may hold values from -0.125 to 0.125
- output_bias: float32 [512], P('blk'), may hold values from -3 to 3
- out_grad: bfloat16 [16384, 512], P('pts', 'blk'), may hold values from -8 to 8
Outputs:
- block_out: bfloat16 [16384, 512], P('pts', 'blk')
- grad_points: float32 [16384, 512], P('pts', 'blk')
- grad_conv_weight: float32 [27, 512, 512], P(None, 'blk', 'pts')
- grad_conv_bias: float32 [512], P('blk')
- grad_cpe_weight: float32 [512, 512], P('blk', 'pts')
- grad_cpe_bias: float32 [512], P('blk')
- grad_cpe_gain: float32 [512], P('blk')
- grad_cpe_shift: float32 [512], P('blk')
- grad_first_gain: float32 [512], P('blk')
- grad_first_shift: float32 [512], P('blk')
- grad_qkv_weight: float32 [512, 3, 512], P('pts', None, 'blk')
- grad_query_value_bias: float32 [2, 512], P(None, 'blk')
- grad_proj_weight: float32 [512, 512], P('blk', 'pts')
- grad_proj_bias: float32 [512], P('blk')
- grad_second_gain: float32 [512], P('blk')
- grad_second_shift: float32 [512], P('blk')
- grad_hidden_weight: float32 [512, 2048], P('pts', 'blk')
- grad_hidden_bias: float32 [2048], P('blk')
- grad_output_weight: float32 [2048, 512], P('blk', 'pts')
- grad_output_bias: float32 [512], P('blk')
Inputs may be any that keep to these rules, and one draw needn't show every extreme that they name: Each neighbour lies at most 256 positions from its own point; in every draw some neighbours lie exactly 256 positions before and after their point. `patch_ids`: patch ids never fall along the points; each patch lies inside one aligned block of 1024 points and holds 1 to 1024 points, some exactly 1024; patches of different indices of pts have different ids.
All inputs are finite; a program needn't handle non-finite values.
Results may differ from a plain program's by a relative error of at most 0.02.
Values may be sent and summed in bfloat16 or wider, within the bound.
No kernel may reach another device: no remote copies, remote signals or barrier semaphores. Data moves between devices by JAX's collectives and lax.ppermute only.
A program may use at most 256 MiB of HBM per device.

v0:
```python
import math

import jax
import jax.numpy as jnp
from jax import lax
from jax.sharding import PartitionSpec as P

HEAD_DIM = 16
PATCH = 1024
KERNEL = 27
REACH = 256


norm_eps = 1e-05
masked_fill = -1e30


def shifted(x, axis, by):
    devices = lax.axis_size(axis)
    pairs = [(i, i + by) for i in range(devices) if 0 <= i + by < devices]
    return lax.ppermute(x, axis, pairs)


def with_halo(block, sides, width):
    for axis, dim in sides:
        count = lax.axis_size(axis)
        forward = [(i, i + 1) for i in range(count - 1)]
        backward = [(target, source) for source, target in forward]
        low = lax.ppermute(
            lax.slice_in_dim(block, block.shape[dim] - width, None, axis=dim), axis, forward
        )
        high = lax.ppermute(lax.slice_in_dim(block, 0, width, axis=dim), axis, backward)
        block = jnp.concatenate([low, block, high], axis=dim)
    return block


def gelu_tanh(values):
    return jax.nn.gelu(values, approximate=True)


def widen(values):
    return lax.all_gather(values, "blk", axis=1, tiled=True)


def widen_again(values):
    return lax.all_gather(values, "blk", axis=1, tiled=True)


def narrow(partial_sum):
    return lax.psum_scatter(partial_sum, "blk", scatter_dimension=1, tiled=True)


def row_totals(first_sum, second_sum):
    return lax.psum((first_sum, second_sum), "blk")


def pass_back(values, offset):
    return shifted(values.astype(jnp.bfloat16), "pts", offset).astype(values.dtype)


def norm_forward(rows_in, gain_row, shifts):
    widths = rows_in.shape[1] * lax.axis_size("blk")
    totals, squares = row_totals(jnp.sum(rows_in, axis=1), jnp.sum(rows_in * rows_in, axis=1))
    average = totals / widths
    spread = squares / widths - average * average
    scaling = lax.rsqrt(spread + norm_eps)
    normed = (rows_in - average[:, None]) * scaling[:, None]
    return (normed, scaling, normed * gain_row + shifts)


def norm_backward(upstream, normed, scaling, gain_row):
    widths = upstream.shape[1] * lax.axis_size("blk")
    scaled = upstream * gain_row
    totals, inner_sum = row_totals(jnp.sum(scaled, axis=1), jnp.sum(scaled * normed, axis=1))
    result = scaling[:, None] * (
        scaled - totals[:, None] / widths - normed * (inner_sum[:, None] / widths)
    )
    return (result, jnp.sum(upstream * normed, axis=0), jnp.sum(upstream, axis=0))


def block_scores(query_rows, key_rows, patch_row):
    factor = query_rows.shape[2] ** (-0.5)
    scores = (
        jnp.einsum("qhe,khe->hqk", query_rows, key_rows, preferred_element_type=jnp.float32)
        * factor
    )
    same_patch = patch_row[:, None] == patch_row[None, :]
    return jnp.where(same_patch[None], scores, masked_fill)


def attend_forward(pieces):
    triple_rows, patch_row = pieces
    value_rows = triple_rows[:, 2]
    scores = block_scores(triple_rows[:, 0], triple_rows[:, 1], patch_row)
    highest = jnp.max(scores, axis=2, keepdims=True)
    weights = jnp.exp(scores - highest)
    totals = jnp.sum(weights, axis=2, keepdims=True)
    probability = (weights / totals).astype(jnp.bfloat16)
    mixture = jnp.einsum(
        "hqk,khe->qhe", probability, value_rows, preferred_element_type=jnp.float32
    )
    return (mixture.astype(jnp.bfloat16), (highest + jnp.log(totals))[:, :, 0])


def attend_backward(pieces):
    triple_rows, patch_row, log_totals, upstream = pieces
    query_rows = triple_rows[:, 0]
    key_rows = triple_rows[:, 1]
    value_rows = triple_rows[:, 2]
    factor = query_rows.shape[2] ** (-0.5)
    scores = block_scores(query_rows, key_rows, patch_row)
    probability = jnp.exp(scores - log_totals[:, :, None])
    prob_low = probability.astype(jnp.bfloat16)
    grad_values = jnp.einsum("hqk,qhe->khe", prob_low, upstream, preferred_element_type=jnp.float32)
    grad_prob = jnp.einsum("qhe,khe->hqk", upstream, value_rows, preferred_element_type=jnp.float32)
    inner_sum = jnp.sum(probability * grad_prob, axis=2, keepdims=True)
    grad_scores = (probability * (grad_prob - inner_sum)).astype(jnp.bfloat16)
    grad_queries = (
        jnp.einsum("hqk,khe->qhe", grad_scores, key_rows, preferred_element_type=jnp.float32)
        * factor
    )
    grad_keys = (
        jnp.einsum("hqk,qhe->khe", grad_scores, query_rows, preferred_element_type=jnp.float32)
        * factor
    )
    return jnp.stack([grad_queries, grad_keys, grad_values], axis=1).astype(jnp.bfloat16)


def pick_table(local_index, span):
    places = jnp.arange(span, dtype=jnp.int32)[None, None, :]
    return (local_index[:, :, None] == places).astype(jnp.bfloat16)


def shards(
    points,
    neighbours,
    patch_ids,
    conv_weight,
    conv_bias,
    cpe_weight,
    cpe_bias,
    cpe_gain,
    cpe_shift,
    first_gain,
    first_shift,
    qkv_weight,
    query_value_bias,
    proj_weight,
    proj_bias,
    second_gain,
    second_shift,
    hidden_weight,
    hidden_bias,
    output_weight,
    output_bias,
    out_grad,
):
    row_count = points.shape[0]
    local_width = points.shape[1]
    head_count = qkv_weight.shape[2] // HEAD_DIM
    block_count = row_count // PATCH
    row_block = math.gcd(row_count, 128)
    pick_count = row_count // row_block
    span = row_block + 2 * REACH
    starts = jnp.arange(pick_count, dtype=jnp.int32) * row_block
    padded = with_halo(points, (("pts", 0),), REACH)
    lookup = neighbours - lax.axis_index("pts") * row_count + REACH
    lookup_blocks = lookup.reshape(pick_count, row_block, KERNEL) - starts[:, None, None]

    def pick_rows(pieces):
        start, local_index = pieces
        window = lax.dynamic_slice_in_dim(padded, start, span, 0)
        table = pick_table(local_index, span)
        return jnp.einsum("bks,sc->bkc", table, window, preferred_element_type=jnp.float32).astype(
            jnp.bfloat16
        )

    kernel_rows = conv_weight.reshape(KERNEL * local_width, conv_weight.shape[2])
    gathered = lax.map(pick_rows, (starts, lookup_blocks)).reshape(row_count, KERNEL * local_width)
    conv_part = narrow(jnp.dot(gathered, kernel_rows, preferred_element_type=jnp.float32))
    conv_low = (conv_part + conv_bias).astype(jnp.bfloat16)
    cpe_pre = narrow(jnp.dot(conv_low, cpe_weight, preferred_element_type=jnp.float32)) + cpe_bias
    normed_cpe, scaling_cpe, cpe_out = norm_forward(cpe_pre, cpe_gain, cpe_shift)
    residual_one = points.astype(jnp.float32) + cpe_out
    normed_one, scaling_one, layer_one = norm_forward(residual_one, first_gain, first_shift)
    low_one = layer_one.astype(jnp.bfloat16)
    wide_one = widen(low_one)
    bias_full = jnp.stack(
        [query_value_bias[0], jnp.zeros_like(query_value_bias[0]), query_value_bias[1]], axis=0
    )
    triple = (
        jnp.einsum("rd,dtc->rtc", wide_one, qkv_weight, preferred_element_type=jnp.float32)
        + bias_full
    ).astype(jnp.bfloat16)
    shaped = triple.reshape(block_count, PATCH, 3, head_count, HEAD_DIM)
    patch_blocks = patch_ids.reshape(block_count, PATCH)
    attended, log_totals = lax.map(attend_forward, (shaped, patch_blocks))
    attended = attended.reshape(row_count, local_width)
    proj_part = narrow(jnp.dot(attended, proj_weight, preferred_element_type=jnp.float32))
    residual_two = residual_one + proj_part + proj_bias
    normed_two, scaling_two, layer_two = norm_forward(residual_two, second_gain, second_shift)
    low_two = layer_two.astype(jnp.bfloat16)
    wide_two = widen(low_two)
    hidden_pre = jnp.dot(wide_two, hidden_weight, preferred_element_type=jnp.float32) + hidden_bias
    activated, gelu_back = jax.vjp(gelu_tanh, hidden_pre)
    act_low = activated.astype(jnp.bfloat16)
    mlp_part = narrow(jnp.dot(act_low, output_weight, preferred_element_type=jnp.float32))
    block_out = (residual_two + mlp_part + output_bias).astype(jnp.bfloat16)
    grad_wide = widen(out_grad)
    upstream = out_grad.astype(jnp.float32)
    grad_output_bias = jnp.sum(upstream, axis=0)
    grad_output_weight = jnp.einsum(
        "rf,rd->fd", act_low, grad_wide, preferred_element_type=jnp.float32
    )
    grad_act = jnp.einsum("rd,fd->rf", grad_wide, output_weight, preferred_element_type=jnp.float32)
    grad_pre = gelu_back(grad_act)[0]
    grad_hidden_bias = jnp.sum(grad_pre, axis=0)
    pre_low = grad_pre.astype(jnp.bfloat16)
    wide_two = widen_again(low_two)
    grad_hidden_weight = jnp.einsum(
        "rd,rf->df", wide_two, pre_low, preferred_element_type=jnp.float32
    )
    grad_layer_two = narrow(
        jnp.einsum("rf,df->rd", pre_low, hidden_weight, preferred_element_type=jnp.float32)
    )
    back_two, grad_second_gain, grad_second_shift = norm_backward(
        grad_layer_two, normed_two, scaling_two, second_gain
    )
    grad_res_two = upstream + back_two
    grad_proj_bias = jnp.sum(grad_res_two, axis=0)
    res_two_wide = widen(grad_res_two.astype(jnp.bfloat16))
    grad_proj_weight = jnp.einsum(
        "rc,rd->cd", attended, res_two_wide, preferred_element_type=jnp.float32
    )
    grad_attended = jnp.einsum(
        "rd,cd->rc", res_two_wide, proj_weight, preferred_element_type=jnp.float32
    ).astype(jnp.bfloat16)
    grad_blocks = grad_attended.reshape(block_count, PATCH, head_count, HEAD_DIM)
    grad_triple = lax.map(attend_backward, (shaped, patch_blocks, log_totals, grad_blocks))
    grad_triple = grad_triple.reshape(row_count, 3, local_width)
    grad_query_value_bias = jnp.stack(
        [
            jnp.sum(grad_triple[:, 0], axis=0, dtype=jnp.float32),
            jnp.sum(grad_triple[:, 2], axis=0, dtype=jnp.float32),
        ],
        axis=0,
    )
    wide_one = widen_again(low_one)
    grad_qkv_weight = jnp.einsum(
        "rd,rtc->dtc", wide_one, grad_triple, preferred_element_type=jnp.float32
    )
    grad_layer_one = narrow(
        jnp.einsum("rtc,dtc->rd", grad_triple, qkv_weight, preferred_element_type=jnp.float32)
    )
    back_one, grad_first_gain, grad_first_shift = norm_backward(
        grad_layer_one, normed_one, scaling_one, first_gain
    )
    grad_res_one = grad_res_two + back_one
    grad_cpe_pre, grad_cpe_gain, grad_cpe_shift = norm_backward(
        grad_res_one, normed_cpe, scaling_cpe, cpe_gain
    )
    grad_cpe_bias = jnp.sum(grad_cpe_pre, axis=0)
    cpe_wide = widen(grad_cpe_pre.astype(jnp.bfloat16))
    grad_cpe_weight = jnp.einsum(
        "rc,rd->cd", conv_low, cpe_wide, preferred_element_type=jnp.float32
    )
    grad_conv_mid = jnp.einsum(
        "rd,cd->rc", cpe_wide, cpe_weight, preferred_element_type=jnp.float32
    )
    grad_conv_bias = jnp.sum(grad_conv_mid, axis=0)
    conv_wide = widen(grad_conv_mid.astype(jnp.bfloat16))
    grad_conv_weight = jnp.einsum(
        "rk,rd->kd", gathered, conv_wide, preferred_element_type=jnp.float32
    )
    grad_conv_weight = grad_conv_weight.reshape(KERNEL, local_width, grad_conv_weight.shape[1])
    grad_gathered = jnp.einsum(
        "rd,kd->rk", conv_wide, kernel_rows, preferred_element_type=jnp.float32
    )
    grad_gathered = grad_gathered.reshape(pick_count, row_block, KERNEL, local_width)

    def spread_rows(carry, pieces):
        start, local_index, grads = pieces
        table = pick_table(local_index, span)
        upper = grads.astype(jnp.bfloat16)
        lower = (grads - upper.astype(jnp.float32)).astype(jnp.bfloat16)
        part = jnp.einsum("bks,bkc->sc", table, upper, preferred_element_type=jnp.float32)
        part = part + jnp.einsum("bks,bkc->sc", table, lower, preferred_element_type=jnp.float32)
        current = lax.dynamic_slice_in_dim(carry, start, span, 0)
        return (lax.dynamic_update_slice_in_dim(carry, current + part, start, 0), None)

    grad_padded = jnp.zeros((padded.shape[0], local_width), jnp.float32)
    grad_padded, unused = lax.scan(spread_rows, grad_padded, (starts, lookup_blocks, grad_gathered))
    from_above = pass_back(grad_padded[:REACH], -1)
    from_below = pass_back(grad_padded[row_count + REACH :], 1)
    grad_points = grad_res_one + grad_padded[REACH : REACH + row_count]
    grad_points = grad_points.at[row_count - REACH :].add(from_above)
    grad_points = grad_points.at[:REACH].add(from_below)
    sum_conv, sum_cpe, sum_qkv, sum_proj, sum_hidden, sum_output = (
        lax.psum_scatter(
            grad_conv_weight.astype(jnp.bfloat16), "pts", scatter_dimension=2, tiled=True
        ).astype(jnp.float32),
        lax.psum_scatter(
            grad_cpe_weight.astype(jnp.bfloat16), "pts", scatter_dimension=1, tiled=True
        ).astype(jnp.float32),
        lax.psum_scatter(
            grad_qkv_weight.astype(jnp.bfloat16), "pts", scatter_dimension=0, tiled=True
        ).astype(jnp.float32),
        lax.psum_scatter(
            grad_proj_weight.astype(jnp.bfloat16), "pts", scatter_dimension=1, tiled=True
        ).astype(jnp.float32),
        lax.psum_scatter(
            grad_hidden_weight.astype(jnp.bfloat16), "pts", scatter_dimension=0, tiled=True
        ).astype(jnp.float32),
        lax.psum_scatter(
            grad_output_weight.astype(jnp.bfloat16), "pts", scatter_dimension=1, tiled=True
        ).astype(jnp.float32),
    )
    (
        bias_conv,
        bias_cpe,
        gain_cpe,
        shift_cpe,
        gain_one,
        shift_one,
        bias_query_value,
        bias_proj,
        gain_two,
        shift_two,
        bias_hidden,
        bias_output,
    ) = lax.psum(
        (
            grad_conv_bias,
            grad_cpe_bias,
            grad_cpe_gain,
            grad_cpe_shift,
            grad_first_gain,
            grad_first_shift,
            grad_query_value_bias,
            grad_proj_bias,
            grad_second_gain,
            grad_second_shift,
            grad_hidden_bias,
            grad_output_bias,
        ),
        "pts",
    )
    return (
        block_out,
        grad_points,
        sum_conv,
        bias_conv,
        sum_cpe,
        bias_cpe,
        gain_cpe,
        shift_cpe,
        gain_one,
        shift_one,
        sum_qkv,
        bias_query_value,
        sum_proj,
        bias_proj,
        gain_two,
        shift_two,
        sum_hidden,
        bias_hidden,
        sum_output,
        bias_output,
    )


def solution(mesh):
    return jax.shard_map(
        shards,
        mesh=mesh,
        in_specs=(
            P("pts", "blk"),
            P("pts", None),
            P("pts"),
            P(None, "blk", None),
            P("blk"),
            P("blk", None),
            P("blk"),
            P("blk"),
            P("blk"),
            P("blk"),
            P("blk"),
            P(None, None, "blk"),
            P(None, "blk"),
            P("blk", None),
            P("blk"),
            P("blk"),
            P("blk"),
            P(None, "blk"),
            P("blk"),
            P("blk", None),
            P("blk"),
            P("pts", "blk"),
        ),
        out_specs=(
            P("pts", "blk"),
            P("pts", "blk"),
            P(None, "blk", "pts"),
            P("blk"),
            P("blk", "pts"),
            P("blk"),
            P("blk"),
            P("blk"),
            P("blk"),
            P("blk"),
            P("pts", None, "blk"),
            P(None, "blk"),
            P("blk", "pts"),
            P("blk"),
            P("blk"),
            P("blk"),
            P("pts", "blk"),
            P("blk"),
            P("blk", "pts"),
            P("blk"),
        ),
        check_vma=False,
    )
```

profile of v0, /device:TPU:5, one launch (start us, length us, event | category | flops | bytes accessed | tf_op | source)
XLA Modules:
  0.0 1602.1 jit_solution(4926397799029735501)
XLA Ops:
  20.3 111.4 %while.44 = (s32[]{:T(128)}, bf16[16,128,27,128]{3,1,2,0:T(8,128)(2,1)}, s32[16,128,27]{1,2,0:T(8,128)}, s32[16]{0:T(128)S(1)}, bf16[2560,128]{1,0:T(8,128)(2,1)}, /*index=5*/s32[]{:T(128)}, s32[]{:T(128)}, s32[]{:T(128)}) while((s32[]{:T(128)}, bf16[16,128,27,128]{3,1,2,0:T(8,128)(2,1)}, s32[16,128,27]{1,2,0:T(8,128)}, s32[16]{0:T(128)S(1)}, ...), condition=%wide.region_1.2_spmd, body=%wide.region_0.1_spmd.sunk | while | flops 568885248 | bytes 1090199 | solution.py:179
  131.8 19.0 %copy.56 = bf16[16,128,27,128]{1,0,3,2:T(8,128)(2,1)} copy(bf16[16,128,27,128]{3,1,2,0:T(8,128)(2,1)} %get-tuple-element.158) | data formatting | bytes 28311552 | tf_op jit(solution)/shard_map/while | solution.py:179
  150.7 12.3 fusion.74
  163.1 46.3 %reduce-scatter.13.cloned.1.call-done = f32[2048,128]{1,0:T(8,128)} async-done(((f32[2048,512]{1,0:T(8,128)}), f32[2048,128]{1,0:T(8,128)}) %reduce-scatter.13.cloned.1.call-update) | async-done | bytes 1048592 | tf_op jit(solution)/shard_map/reduce_scatter | solution.py:50
  213.4 44.7 %reduce-scatter.15.cloned.1.call-done = f32[2048,128]{1,0:T(8,128)} async-done(((f32[2048,512]{1,0:T(8,128)}), f32[2048,128]{1,0:T(8,128)}) %reduce-scatter.15.cloned.1.call-update) | async-done | bytes 1048592 | tf_op jit(solution)/shard_map/reduce_scatter | solution.py:50
  259.9 10.3 all-reduce.6
  274.6 10.8 all-reduce.5
  291.3 23.0 %all-gather.7.cloned.1.call-done = bf16[2048,512]{1,0:T(8,128)(2,1)} async-done(((bf16[2048,128]{1,0:T(8,128)(2,1)}), bf16[2048,512]{1,0:T(8,128)(2,1)}) %all-gather.7.cloned.1.call-update) | async-done | bytes 2097168 | tf_op jit(solution)/shard_map/all_gather | solution.py:42
  327.9 90.4 %while.45 = (s32[]{:T(128)}, bf16[2,1024,8,16]{1,3,2,0:T(8,128)(2,1)}, f32[2,8,1024]{2,1,0:T(8,128)}, bf16[2,1024,3,8,16]{1,4,3,2,0:T(8,128)(2,1)}, s32[2,1024]{1,0:T(2,128)S(1)}, /*index=5*/s32[]{:T(128)}) while((s32[]{:T(128)}, bf16[2,1024,8,16]{1,3,2,0:T(8,128)(2,1)}, f32[2,8,1024]{2,1,0:T(8,128)}, ...), condition=%wide.region_15.16_spmd, body=%wide.region_12.15_spmd.sunk | while | flops 638705664 | bytes 112472272 | solution.py:197
  329.7 13.5 fusion.135
  343.3 14.2 fusion.136
  357.5 14.1 fusion.137
  374.9 13.5 fusion.135
  388.5 14.2 fusion.136
  402.8 14.1 fusion.137
  424.4 44.2 %reduce-scatter.17.cloned.1.call-done = f32[2048,128]{1,0:T(8,128)} async-done(((f32[2048,512]{1,0:T(8,128)}), f32[2048,128]{1,0:T(8,128)}) %reduce-scatter.17.cloned.1.call-update) | async-done | bytes 1048592 | tf_op jit(solution)/shard_map/reduce_scatter | solution.py:50
  472.2 10.9 all-reduce.4
  488.1 23.8 %all-gather.9.cloned.1.call-done = bf16[2048,512]{1,0:T(8,128)(2,1)} async-done(((bf16[2048,128]{1,0:T(8,128)(2,1)}), bf16[2048,512]{1,0:T(8,128)(2,1)}) %all-gather.9.cloned.1.call-update) | async-done | bytes 2097168 | tf_op jit(solution)/shard_map/all_gather | solution.py:42
  516.8 19.5 %all-gather.11.cloned.1.call-done = bf16[2048,512]{1,0:T(8,128)(2,1)} async-done(((bf16[2048,128]{1,0:T(8,128)(2,1)}), bf16[2048,512]{1,0:T(8,128)(2,1)}) %all-gather.11.cloned.1.call-update) | async-done | bytes 2097168 | tf_op jit(solution)/shard_map/all_gather | solution.py:42
  554.7 38.0 %reduce-scatter.21.cloned.1.call-done = f32[2048,128]{1,0:T(8,128)} async-done(((f32[2048,512]{1,0:T(8,128)}), f32[2048,128]{1,0:T(8,128)}) %reduce-scatter.21.cloned.1.call-update) | async-done | bytes 1048592 | tf_op jit(solution)/shard_map/reduce_scatter | solution.py:50
  595.8 11.0 all-reduce.3
  608.1 31.6 %reduce-scatter.19.cloned.1.call-done = f32[2048,128]{1,0:T(8,128)} async-done(((f32[2048,512]{1,0:T(8,128)}), f32[2048,128]{1,0:T(8,128)}) %reduce-scatter.19.cloned.1.call-update) | async-done | bytes 1048592 | tf_op jit(solution)/shard_map/reduce_scatter | solution.py:50
  646.9 23.4 %all-gather.13.cloned.1.call-done = bf16[2048,512]{1,0:T(8,128)(2,1)} async-done(((bf16[2048,128]{1,0:T(8,128)(2,1)}), bf16[2048,512]{1,0:T(8,128)(2,1)}) %all-gather.13.cloned.1.call-update) | async-done | bytes 2097168 | tf_op jit(solution)/shard_map/all_gather | solution.py:42
  679.6 215.3 %while.46 = (s32[]{:T(128)}, bf16[2,1024,3,8,16]{1,4,3,2,0:T(8,128)(2,1)}, bf16[2,1024,3,8,16]{1,4,3,2,0:T(8,128)(2,1)}, s32[2,1024]{1,0:T(2,128)S(1)}, f32[2,8,...) while((s32[]{:T(128)}, bf16[2,1024,3,8,16]{1,4,3,2,0:T(8,128)(2,1)}, ...), condition=%wide.region_29.30_spmd, body=%wide.region_27.29_spmd.sunk | while | flops 1472061440 | bytes 266055856 | solution.py:239
  684.0 13.1 fusion.142
  697.1 15.4 fusion.143
  712.5 26.3 %multiply_reduce_fusion.14 = (f32[8,1024]{1,0:T(8,128)}, f32[8,1024,1024]{1,2,0:T(8,128)}) fusion(f32[8,1024,1024]{1,2,0:T(8,128)} %fusion.142, f32[8,1024]{1,0:T(8,128)} %dynamic-slice_bitcast_fusion.13, pred[1024,1024]{0,1:T(8,128)(4,1)} %broadcast_compare_fusion.5, bf16[1024,3,8,16]{0,3,2,1:T(8,128)(2,1)} %copy-done.1, ...), kind=kOutput, calls=%fused_computation.30.clone.1 | convolution fusion | flops 310370304 | bytes 68747264 | tf_op jit(solution)/shard_map/while/body/eval_jaxpr/qhe,khe->hqk/dot_general | solution.py:115
  738.8 28.8 %multiply_convert_fusion.5 = bf16[8,1024,1024]{1,2,0:T(8,128)(2,1)} fusion(f32[8,1024,1024]{1,2,0:T(8,128)} %get-tuple-element.448, f32[8,1024,1024]{1,2,0:T(8,128)} %fusion.142, f32[8,1024]{1,0:T(8,128)} %get-tuple-element.449, f32[8,1024]{1,0:T(8,128)} %dynamic-slice_bitcast_fusion.13, pred[1024,1024]{0,1:T(8,128)(4,1)} %broadcast_compare_fusion.5), kind=kLoop, calls=%fused_computation.29.clone.1 | loop fusion | flops 50331648 | bytes 85000192 | tf_op jit(solution)/shard_map/while/body/eval_jaxpr/convert_element_type | solution.py:117
  775.8 10.4 fusion.144
  791.4 13.1 fusion.142
  804.5 15.4 fusion.143
  819.9 26.3 %multiply_reduce_fusion.14 = (f32[8,1024]{1,0:T(8,128)}, f32[8,1024,1024]{1,2,0:T(8,128)}) fusion(f32[8,1024,1024]{1,2,0:T(8,128)} %fusion.142, f32[8,1024]{1,0:T(8,128)} %dynamic-slice_bitcast_fusion.13, pred[1024,1024]{0,1:T(8,128)(4,1)} %broadcast_compare_fusion.5, bf16[1024,3,8,16]{0,3,2,1:T(8,128)(2,1)} %copy-done.1, ...), kind=kOutput, calls=%fused_computation.30.clone.1 | convolution fusion | flops 310370304 | bytes 68747264 | tf_op jit(solution)/shard_map/while/body/eval_jaxpr/qhe,khe->hqk/dot_general | solution.py:115
  846.2 28.8 %multiply_convert_fusion.5 = bf16[8,1024,1024]{1,2,0:T(8,128)(2,1)} fusion(f32[8,1024,1024]{1,2,0:T(8,128)} %get-tuple-element.448, f32[8,1024,1024]{1,2,0:T(8,128)} %fusion.142, f32[8,1024]{1,0:T(8,128)} %get-tuple-element.449, f32[8,1024]{1,0:T(8,128)} %dynamic-slice_bitcast_fusion.13, pred[1024,1024]{0,1:T(8,128)(4,1)} %broadcast_compare_fusion.5), kind=kLoop, calls=%fused_computation.29.clone.1 | loop fusion | flops 50331648 | bytes 85000192 | tf_op jit(solution)/shard_map/while/body/eval_jaxpr/convert_element_type | solution.py:117
  883.2 10.4 fusion.144
  907.7 44.2 %reduce-scatter.23.cloned.1.call-done = f32[2048,128]{1,0:T(8,128)} async-done(((f32[2048,512]{1,0:T(8,128)}), f32[2048,128]{1,0:T(8,128)}) %reduce-scatter.23.cloned.1.call-update) | async-done | bytes 1048592 | tf_op jit(solution)/shard_map/reduce_scatter | solution.py:50
  955.1 10.9 all-reduce.2
  973.4 11.5 all-reduce.1
  1022.9 15.9 copy.85
  1038.8 39.5 %reduce-scatter.33.cloned.1.call-done = bf16[64,512]{1,0:T(8,128)(2,1)} async-done(((bf16[512,512]{1,0:T(8,128)(2,1)}), bf16[64,512]{1,0:T(8,128)(2,1)}) %reduce-scatter.33.cloned.1.call-update) | async-done | bytes 65552 | tf_op jit(solution)/shard_map/reduce_scatter | solution.py:311
  1079.8 63.1 %reduce-scatter.35.cloned.1.call-done = bf16[512,64]{0,1:T(8,128)(2,1)} async-done(((bf16[512,512]{0,1:T(8,128)(2,1)}), bf16[512,64]{0,1:T(8,128)(2,1)}) %reduce-scatter.35.cloned.1.call-update) | async-done | bytes 65552 | tf_op jit(solution)/shard_map/reduce_scatter | solution.py:314
  1145.8 60.1 %reduce-scatter.31.cloned.1.call-done = bf16[128,64]{0,1:T(8,128)(2,1)} async-done(((bf16[128,512]{0,1:T(8,128)(2,1)}), bf16[128,64]{0,1:T(8,128)(2,1)}) %reduce-scatter.31.cloned.1.call-update) | async-done | bytes 16400 | tf_op jit(solution)/shard_map/reduce_scatter | solution.py:308
  1207.3 63.0 %reduce-scatter.29.cloned.1.call-done = bf16[64,3,128]{2,0,1:T(8,128)(2,1)} async-done(((bf16[512,3,128]{2,0,1:T(8,128)(2,1)}), bf16[64,3,128]{2,0,1:T(8,128)(2,1)}) %reduce-scatter.29.cloned.1.call-update) | async-done | bytes 49168 | tf_op jit(solution)/shard_map/reduce_scatter | solution.py:305
  1271.7 15.2 all-reduce
  1286.9 46.4 %reduce-scatter.27.cloned.1.call-done = bf16[128,64]{0,1:T(8,128)(2,1)} async-done(((bf16[128,512]{0,1:T(8,128)(2,1)}), bf16[128,64]{0,1:T(8,128)(2,1)}) %reduce-scatter.27.cloned.1.call-update) | async-done | bytes 16400 | tf_op jit(solution)/shard_map/reduce_scatter | solution.py:302
  1334.7 25.0 %all-gather.17.cloned.1.call-done = bf16[2048,512]{1,0:T(8,128)(2,1)} async-done(((bf16[2048,128]{1,0:T(8,128)(2,1)}), bf16[2048,512]{1,0:T(8,128)(2,1)}) %all-gather.17.cloned.1.call-update) | async-done | bytes 2097168 | tf_op jit(solution)/shard_map/all_gather | solution.py:42
  1359.7 12.9 convolution_convert_fusion
  1372.6 14.7 fusion.59
  1388.5 191.2 %while.47 = (s32[]{:T(128)}, f32[2560,128]{1,0:T(8,128)}, s32[16]{0:T(128)S(1)}, s32[16,128,27]{1,2,0:T(8,128)}, f32[16,128,27,128]{3,1,2,0:T(8,128)}, /*index=5*/s32[]{:T(128)}, s32[]{:T(128)}, s32[]{:T(128)}) while((s32[]{:T(128)}, f32[2560,128]{1,0:T(8,128)}, s32[16]{0:T(128)S(1)}, s32[16,128,27]{1,2,0:T(8,128)}, ...), condition=%wide.region_40.41_spmd, body=%wide.region_39.40_spmd.sunk | while | flops 1138819072 | bytes 4675743 | solution.py:292
  (331 shorter events, 461.1 us)
Async XLA Ops:
  7.2 143.5 %copy-start = (bf16[27,128,512]{2,1,0:T(8,128)(2,1)S(1)}, bf16[27,128,512]{2,1,0:T(8,128)(2,1)}, u32[]{:S(2)}) copy-start(bf16[27,128,512]{2,1,0:T(8,128)(2,1)} %param.37) | copy-start | bytes 10616836
  7.2 202.2 %reduce-scatter.13.cloned.1.call-start = ((), (), s32[]{:S(2)}) async-start(), calls=%async_computation.12 | async-start | bytes 5242880 | tf_op jit(solution)/shard_map/reduce_scatter | solution.py:50
  8.9 9.4 collective-permute-start
  12.1 6.3 collective-permute-start.1
  131.7 19.0 %copy-start.23 = (s32[16]{0:T(128)}, s32[16]{0:T(128)S(1)}, u32[]{:S(2)}) copy-start(s32[16]{0:T(128)S(1)} %get-tuple-element.618) | copy-start | bytes 196
  163.0 46.4 %copy-start.21 = (f32[128]{0:T(128)S(1)}, f32[128]{0:T(128)}, u32[]{:S(2)}) copy-start(f32[128]{0:T(128)} %param.38) | copy-start | bytes 1540
  163.1 95.0 %reduce-scatter.15.cloned.1.call-start = ((), (), s32[]{:S(2)}) async-start(), calls=%async_computation.13 | async-start | bytes 5242880 | tf_op jit(solution)/shard_map/reduce_scatter | solution.py:50
  213.3 101.0 %all-gather.7.cloned.1.call-start = ((), (), s32[]{:S(2)}) async-start(), calls=%async_computation.14 | async-start | bytes 2621440 | tf_op jit(solution)/shard_map/all_gather | solution.py:42
  270.9 3.7 copy-start.13
  289.5 179.2 %reduce-scatter.17.cloned.1.call-start = ((), (), s32[]{:S(2)}) async-start(), calls=%async_computation.15 | async-start | bytes 5242880 | tf_op jit(solution)/shard_map/reduce_scatter | solution.py:50
  343.3 14.3 copy-start.7
  357.5 14.1 copy-start.9
  371.6 0.8 copy-start.8
  388.5 14.3 copy-start.7
  402.7 14.1 copy-start.9
  416.8 0.8 copy-start.8
  420.0 0.8 copy-start.5
  424.4 87.6 %all-gather.9.cloned.1.call-start = ((), (), s32[]{:S(2)}) async-start(), calls=%async_computation.16 | async-start | bytes 2621440 | tf_op jit(solution)/shard_map/all_gather | solution.py:42
  487.1 49.2 %all-gather.11.cloned.1.call-start = ((), (), s32[]{:S(2)}) async-start(), calls=%async_computation.18 | async-start | bytes 2621440 | tf_op jit(solution)/shard_map/all_gather | solution.py:42
  487.7 105.0 %reduce-scatter.21.cloned.1.call-start = ((), (), s32[]{:S(2)}) async-start(), calls=%async_computation.19 | async-start | bytes 5242880 | tf_op jit(solution)/shard_map/reduce_scatter | solution.py:50
  536.3 8.8 copy-start.6
  543.8 1.3 copy-start.2
  548.5 91.3 %reduce-scatter.19.cloned.1.call-start = ((), (), s32[]{:S(2)}) async-start(), calls=%async_computation.17 | async-start | bytes 5242880 | tf_op jit(solution)/shard_map/reduce_scatter | solution.py:50
  554.6 115.7 %all-gather.13.cloned.1.call-start = ((), (), s32[]{:S(2)}) async-start(), calls=%async_computation.20 | async-start | bytes 2621440 | tf_op jit(solution)/shard_map/all_gather | solution.py:42
  645.0 1.0 copy-start.3
  646.9 305.1 %reduce-scatter.23.cloned.1.call-start = ((), (), s32[]{:S(2)}) async-start(), calls=%async_computation.21 | async-start | bytes 5242880 | tf_op jit(solution)/shard_map/reduce_scatter | solution.py:50
  682.3 1.6 copy-start.1
  775.8 10.4 copy-start.4
  789.7 1.6 copy-start.1
  883.2 10.4 copy-start.4
  907.7 59.7 %copy-start.12 = (f32[2048]{0:T(1024)S(1)}, f32[2048]{0:T(1024)}, u32[]{:S(2)}) copy-start(f32[2048]{0:T(1024)} %copy-done.11) | copy-start | bytes 24580
  907.7 59.7 %copy-start.14 = (f32[2048]{0:T(1024)S(1)}, f32[2048]{0:T(1024)}, u32[]{:S(2)}) copy-start(f32[2048]{0:T(1024)} %copy-done.13) | copy-start | bytes 24580
  907.7 107.9 %all-gather.15.cloned.1.call-start = ((), (), s32[]{:S(2)}) async-start(), calls=%async_computation.22 | async-start | bytes 2621440 | tf_op jit(solution)/shard_map/all_gather | solution.py:42
  990.7 4.4 copy-start.25
  990.8 87.5 %reduce-scatter.33.cloned.1.call-start = ((), (), s32[]{:S(2)}) async-start(), calls=%async_computation.28 | async-start | bytes 589824 | tf_op jit(solution)/shard_map/reduce_scatter | solution.py:311
  995.1 147.8 %reduce-scatter.35.cloned.1.call-start = ((), (), s32[]{:S(2)}) async-start(), calls=%async_computation.29 | async-start | bytes 589824 | tf_op jit(solution)/shard_map/reduce_scatter | solution.py:314
  1000.9 14.7 copy-start.22
  1000.9 205.1 %reduce-scatter.31.cloned.1.call-start = ((), (), s32[]{:S(2)}) async-start(), calls=%async_computation.27 | async-start | bytes 147456 | tf_op jit(solution)/shard_map/reduce_scatter | solution.py:308
  1004.4 265.9 %reduce-scatter.29.cloned.1.call-start = ((), (), s32[]{:S(2)}) async-start(), calls=%async_computation.26 | async-start | bytes 442368 | tf_op jit(solution)/shard_map/reduce_scatter | solution.py:305
  1008.5 324.8 %reduce-scatter.27.cloned.1.call-start = ((), (), s32[]{:S(2)}) async-start(), calls=%async_computation.25 | async-start | bytes 147456 | tf_op jit(solution)/shard_map/reduce_scatter | solution.py:302
  1019.1 340.6 %all-gather.17.cloned.1.call-start = ((), (), s32[]{:S(2)}) async-start(), calls=%async_computation.23 | async-start | bytes 2621440 | tf_op jit(solution)/shard_map/all_gather | solution.py:42
  1022.8 570.2 %reduce-scatter.25.cloned.1.call-start = ((), (), s32[]{:S(2)}) async-start(), calls=%async_computation.24 | async-start | bytes 3981312 | tf_op jit(solution)/shard_map/reduce_scatter | solution.py:299
  1022.9 248.9 %copy-start.18 = (f32[128]{0:T(128)S(1)}, f32[128]{0:T(128)}, u32[]{:S(2)}) copy-start(f32[128]{0:T(128)} %get-tuple-element.197) | copy-start | bytes 1540
  1022.9 248.9 %copy-start.19 = (f32[128]{0:T(128)S(1)}, f32[128]{0:T(128)}, u32[]{:S(2)}) copy-start(f32[128]{0:T(128)} %get-tuple-element.208) | copy-start | bytes 1540
  1022.9 248.9 %copy-start.20 = (f32[128]{0:T(128)S(1)}, f32[128]{0:T(128)}, u32[]{:S(2)}) copy-start(f32[128]{0:T(128)} %get-tuple-element.283) | copy-start | bytes 1540
  1372.6 15.9 copy-start.24
  1581.0 8.8 collective-permute-start.2
  1585.9 5.6 collective-permute-start.3
  (6 other events, 3.7 us)
Sparse Core Ops, SparseCore 0:
  163.2 46.2 reduce-scatter.12
  213.4 44.5 reduce-scatter.14
  289.6 24.6 all-gather.6
  424.5 44.0 reduce-scatter.16
  487.2 24.7 all-gather.8
  513.4 22.8 all-gather.10
  548.6 44.0 reduce-scatter.20
  595.2 44.4 reduce-scatter.18
  647.0 23.2 all-gather.12
  907.8 44.0 reduce-scatter.22
  990.9 24.6 all-gather.14
  1018.8 59.4 reduce-scatter.32
  1082.0 60.8 reduce-scatter.34
  1146.1 59.8 reduce-scatter.30
  1209.1 61.1 reduce-scatter.28
  1273.5 59.8 reduce-scatter.26
  1335.3 24.3 all-gather.16
  1372.7 78.7 reduce-scatter.24
where the time goes:
time: 1620 us; the launch traced here: 1600 us
  waiting for transfers between devices  644 us (40%)
  matrix products  475 us (29%)
  other arithmetic  157 us (10%)
  local copies, waits for them, and re-layouts  154 us (10%)
  blocking collectives  80.7 us (5%)
  loops' own time  63.1 us (4%)
    reduce_scatter x6, waiting for transfers between devices, narrow(): return lax.psum_scatter(partial_sum, 'blk', scatter_dimension=1, tiled=True)  249 us
    all_gather x6, waiting for transfers between devices, widen(): return lax.all_gather(values, 'blk', axis=1, tiled=True)  122 us
    psum x6, blocking collectives, row_totals(): return lax.psum((first_sum, second_sum), 'blk')  65.5 us
    reduce_scatter x1, waiting for transfers between devices, shards(): lax.psum_scatter(grad_output_weight.astype(jnp.bfloat16), 'pts', scatter_...  63.1 us
    reduce_scatter x1, waiting for transfers between devices, shards(): lax.psum_scatter(grad_qkv_weight.astype(jnp.bfloat16), 'pts', scatter_dim...  63 us
    dot_general x16, matrix products, spread_rows(): jnp.einsum('bks,bkc->sc', table, lower, preferred_element_type=jnp.float32)  60.8 us
    reduce_scatter x1, waiting for transfers between devices, shards(): lax.psum_scatter(grad_proj_weight.astype(jnp.bfloat16), 'pts', scatter_di...  60.1 us
    dot_general x16, matrix products, pick_rows(): jnp.einsum('bks,sc->bkc', table, window, preferred_element_type=jnp.float32)  59.4 us
  transfers between devices with their start and end apart: 22, of which 17 were waited for; matrix products, arithmetic and copies ran while one was open for 16% of the time, Pallas kernels for 0%

commit v1 on v0

v1 whole, which is shorter than its diff:
```python
import functools
import math

import jax
import jax.numpy as jnp
from jax import lax
from jax.experimental import pallas as pl
from jax.experimental.pallas import tpu as pltpu
from jax.sharding import PartitionSpec as P

HEAD_DIM = 16
PATCH = 1024
KERNEL = 27
REACH = 256
EPS = 1e-05
LOG2E = math.log2(math.e)
BF = jnp.bfloat16
F32 = jnp.float32
VM = pltpu.VMEM
NN = ((1,), (0,))
NT = ((1,), (1,))
TN = ((0,), (0,))


def dot(a, b, dims):
    return lax.dot_general(a, b, (dims, ((), ())), preferred_element_type=F32)


def whole(count):
    return [pl.BlockSpec(memory_space=VM)] * count


def params(mib=48):
    return pltpu.CompilerParams(vmem_limit_bytes=mib * 2**20)


def cost(flops, size=4 * 2**20, exps=0):
    return pl.CostEstimate(flops=int(flops), bytes_accessed=int(size), transcendentals=int(exps))


def struct(shape, kind):
    return jax.ShapeDtypeStruct(shape, kind)


def one_hot(place):
    spots = lax.broadcasted_iota(jnp.int32, (256, 256), 0)
    return jnp.where(spots == jnp.broadcast_to(place, (256, 256)), 1.0, 0.0).astype(BF)


def conv_kernel(window, place, weight, conv, gathered, turned):
    width = window.shape[1]
    for j in range(window.shape[0] // 256):
        turned[j * width : (j + 1) * width, :] = window[j * 256 : (j + 1) * 256, :].T
    for b in range(place.shape[1] // 256):
        cols = slice(b * 256, (b + 1) * 256)
        left = turned[b * width : (b + 3) * width, :]
        for k in range(KERNEL):
            spot = place[k : k + 1, cols]
            part = jnp.broadcast_to(lax.shift_right_logical(spot, 8) - b, (width, 256))
            three = dot(left, one_hot(jnp.bitwise_and(spot, 255)), NN)
            rows = jnp.where(
                part == 0,
                three[:width],
                jnp.where(part == 1, three[width : 2 * width], three[2 * width :]),
            )
            gathered[k * width : (k + 1) * width, cols] = rows.astype(BF)
        conv[cols, :] = dot(gathered[:, cols], weight[...], TN).astype(conv.dtype)


def conv_forward(window, place, weight, kind):
    rows, width, wide = place.shape[1], window.shape[1], weight.shape[1]
    return pl.pallas_call(
        conv_kernel,
        out_shape=(struct((rows, wide), kind), struct((KERNEL * width, rows), BF)),
        in_specs=whole(3),
        out_specs=whole(2),
        scratch_shapes=[pltpu.VMEM((window.shape[0] // 256 * width, 256), BF)],
        compiler_params=params(),
        cost_estimate=cost(4 * rows * KERNEL * width * wide),
        name="conv_forward",
    )(window, place, weight)


def spread_kernel(place, weight, grads, out, upstream):
    width = out.shape[0]
    out[...] = jnp.zeros(out.shape, F32)
    step = 9
    for b in range(place.shape[1] // 256):
        cols = slice(b * 256, (b + 1) * 256)
        upstream[...] = dot(weight[...], grads[cols, :], NT)
        for s in range(KERNEL // step):
            left, right = [], []
            for k in range(s * step, (s + 1) * step):
                spot = place[k : k + 1, cols]
                part = jnp.broadcast_to(lax.shift_right_logical(spot, 8) - b, (width, 256))
                mine = upstream[k * width : (k + 1) * width, :]
                left.append(
                    jnp.concatenate(
                        [jnp.where(part == i, mine, 0.0).astype(BF) for i in range(3)], axis=0
                    )
                )
                right.append(one_hot(jnp.bitwise_and(spot, 255)))
            three = dot(jnp.concatenate(left, axis=1), jnp.concatenate(right, axis=1), NT)
            for i in range(3):
                at = slice((b + i) * 256, (b + i + 1) * 256)
                out[:, at] = out[:, at] + three[i * width : (i + 1) * width]


def spread(place, weight, grads):
    rows, wide = grads.shape
    width = weight.shape[0] // KERNEL
    return pl.pallas_call(
        spread_kernel,
        out_shape=struct((width, rows + 2 * REACH), F32),
        in_specs=whole(3),
        out_specs=pl.BlockSpec(memory_space=VM),
        scratch_shapes=[pltpu.VMEM((KERNEL * width, 256), F32)],
        compiler_params=params(),
        cost_estimate=cost(4 * rows * KERNEL * width * wide),
        name="spread",
    )(place, weight, grads)


def conv_weight_kernel(blocks, *refs):
    gathered, grads, out, turned = refs[:4], refs[4:8], refs[8], refs[9]
    rows = grads[0].shape[0]

    @pl.when(pl.program_id(0) == 0)
    def _():
        for q in range(4):
            turned[:, q * rows : (q + 1) * rows] = grads[q][...].T

    both = jnp.concatenate([g[...] for g in gathered], axis=1)
    total = dot(turned[...], both, NT).astype(BF)
    size = total.shape[0] // blocks
    for p in range(blocks):
        out[p] = total[p * size : (p + 1) * size]


def conv_weight_grad(gathered, grads, first, count, blocks):
    rows, wide = grads[0].shape
    tile = 384
    return pl.pallas_call(
        functools.partial(conv_weight_kernel, blocks),
        grid=(count // tile,),
        out_shape=struct((blocks, wide // blocks, count), BF),
        in_specs=[pl.BlockSpec((tile, rows), lambda i: (i + first // tile, 0))] * 4
        + [pl.BlockSpec((rows, wide), lambda i: (0, 0))] * 4,
        out_specs=pl.BlockSpec((blocks, wide // blocks, tile), lambda i: (0, 0, i)),
        scratch_shapes=[pltpu.VMEM((wide, 4 * rows), BF)],
        compiler_params=params(),
        cost_estimate=cost(8 * rows * wide * count),
        name="conv_weight_grad",
    )(*gathered, *grads)


def split3(values):
    high = values.astype(BF)
    rest = values - high.astype(F32)
    middle = rest.astype(BF)
    return high, middle, (rest - middle.astype(F32)).astype(BF)


def three_rows(high, middle, low):
    spots = lax.broadcasted_iota(jnp.int32, (16, high.shape[1]), 0)
    picked = jnp.where(
        spots == 0,
        high.astype(F32),
        jnp.where(spots == 1, middle.astype(F32), jnp.where(spots == 2, low.astype(F32), 0.0)),
    )
    return picked.astype(BF)


def one_rows(length, count):
    spots = lax.broadcasted_iota(jnp.int32, (16, length), 0)
    return jnp.where(spots < count, 1.0, 0.0).astype(BF)


def patch_codes(patch):
    shape = (32, patch.shape[1])
    spots = lax.broadcasted_iota(jnp.int32, shape, 0)
    bits = jnp.bitwise_and(
        lax.shift_right_logical(jnp.broadcast_to(patch, shape), jnp.bitwise_and(spots, 15)), 1
    )
    bits = jnp.where(spots < 16, bits, 1 - bits)
    return jnp.where(bits == 1, 1.0, 0.0).astype(BF), jnp.where(bits == 1, 0.0, -1e30).astype(BF)


def fixed_rows(patch, query_side, key_side):
    length = patch.shape[1]
    left, right = patch_codes(patch)
    key_side[48:64, :] = one_rows(length, 3)
    key_side[64:96, :] = left
    query_side[64:96, :] = right
    key_side[96:128, :] = jnp.zeros((32, length), BF)
    query_side[96:128, :] = jnp.zeros((32, length), BF)


def attend_forward_kernel(
    heads, tile, mine, other, weight, bias, patch, triple, total, keep, send, logs, query_side, key_side, value_side
):
    rows = mine.shape[0]
    length = 2 * rows
    for t in range(3):
        at = slice(t * weight.shape[0] // 3, (t + 1) * weight.shape[0] // 3)
        triple[t, :, :rows] = (dot(weight[at, :], mine[...], NT) + bias[at, :]).astype(BF)
        triple[t, :, rows:] = (dot(weight[at, :], other[...], NT) + bias[at, :]).astype(BF)
    fixed_rows(patch[...], query_side, key_side)
    value_side[16:32, :] = one_rows(length, 1)

    @pl.loop(0, heads)
    def _(h):
        at = pl.ds(pl.multiple_of(h * HEAD_DIM, HEAD_DIM), HEAD_DIM)
        query = triple[0, at, :].astype(F32) * (HEAD_DIM**-0.5 * LOG2E)
        key = triple[1, at, :]
        high, middle, low = split3(query)
        query_side[0:16, :] = high
        query_side[16:32, :] = middle
        query_side[32:48, :] = low
        query_side[48:64, :] = jnp.zeros((16, length), BF)
        key_side[0:16, :] = key
        key_side[16:32, :] = key
        key_side[32:48, :] = key
        value_side[0:16, :] = triple[2, at, :]
        wide_key = key.astype(F32)
        bound = jnp.max(jnp.sum(query * query, axis=0)) * jnp.max(
            jnp.sum(wide_key * wide_key, axis=0)
        )
        logs[pl.ds(h, 1), :] = jnp.zeros((1, length), F32)

        @pl.when(jnp.logical_not(bound < 4096.0))
        def _():
            for t in range(length // tile):
                cols = slice(t * tile, (t + 1) * tile)
                top = jnp.max(dot(key_side[...], query_side[:, cols], TN), axis=0, keepdims=True)
                query_side[48:64, cols] = three_rows(*split3(-top))
                logs[pl.ds(h, 1), cols] = top

        for t in range(length // tile):
            cols = slice(t * tile, (t + 1) * tile)
            weights = jnp.exp2(dot(key_side[...], query_side[:, cols], TN)).astype(BF)
            mixed = dot(value_side[...], weights, NN)
            sums = mixed[16:17, :]
            mixed = mixed[0:16, :] * (1.0 / sums)
            total[at, cols] = mixed
            if t * tile < rows:
                keep[at, cols] = mixed.astype(BF)
            else:
                send[at, t * tile - rows : (t + 1) * tile - rows] = mixed.astype(BF)
            logs[pl.ds(h, 1), cols] = logs[pl.ds(h, 1), cols] + jnp.log2(sums)


def attend_forward(mine, other, weight, bias, patch):
    rows, length = mine.shape[0], 2 * mine.shape[0]
    width = weight.shape[0] // 3
    heads = width // HEAD_DIM
    return pl.pallas_call(
        functools.partial(attend_forward_kernel, heads, 512),
        out_shape=(
            struct((3, width, length), BF),
            struct((width, length), F32),
            struct((width, rows), BF),
            struct((width, rows), BF),
            struct((heads, length), F32),
        ),
        in_specs=whole(5),
        out_specs=whole(5),
        scratch_shapes=[
            pltpu.VMEM((128, length), BF),
            pltpu.VMEM((128, length), BF),
            pltpu.VMEM((32, length), BF),
        ],
        compiler_params=params(),
        cost_estimate=cost(heads * length * length * 1200, 6 * 2**20, heads * length * length),
        name="attend_forward",
    )(mine, other, weight, bias, patch)


def attend_backward_kernel(
    heads, tile, triple, patch, mine, other, mixed, logs, out, query_side, key_side, value_side, grad_side, grad_value, grad_key
):
    length = triple.shape[2]
    fixed_rows(patch[...], query_side, key_side)
    value_side[16:32, :] = one_rows(length, 3)

    @pl.loop(0, heads)
    def _(h):
        at = pl.ds(pl.multiple_of(h * HEAD_DIM, HEAD_DIM), HEAD_DIM)
        query, key = triple[0, at, :], triple[1, at, :]
        upstream = jnp.concatenate([mine[at, :], other[at, :]], axis=1)
        high, middle, low = split3(query.astype(F32) * (HEAD_DIM**-0.5 * LOG2E))
        query_side[0:16, :] = high
        query_side[16:32, :] = middle
        query_side[32:48, :] = low
        query_side[48:64, :] = three_rows(*split3(-logs[pl.ds(h, 1), :]))
        key_side[0:16, :] = key
        key_side[16:32, :] = key
        key_side[32:48, :] = key
        value_side[0:16, :] = triple[2, at, :]
        inner = jnp.sum(upstream.astype(F32) * mixed[at, :], axis=0, keepdims=True)
        grad_side[0:16, :] = upstream
        grad_side[16:32, :] = three_rows(*split3(-inner))
        for t in range(length // tile):
            cols = slice(t * tile, (t + 1) * tile)
            prob = jnp.exp2(dot(query_side[:, cols], key_side[...], TN))
            grad_prob = dot(grad_side[:, cols], value_side[...], TN)
            grad_score = (prob * grad_prob).astype(BF)
            value_part = dot(upstream[:, cols], prob.astype(BF), NN)
            key_part = dot(query[:, cols], grad_score, NN)
            out[0, at, cols] = (dot(key, grad_score, NT) * HEAD_DIM**-0.5).astype(BF)
            if t == 0:
                grad_value[...] = value_part
                grad_key[...] = key_part
            else:
                grad_value[...] += value_part
                grad_key[...] += key_part
        out[1, at, :] = (grad_key[...] * HEAD_DIM**-0.5).astype(BF)
        out[2, at, :] = grad_value[...].astype(BF)


def attend_backward(triple, patch, mine, other, mixed, logs):
    width, length = triple.shape[1:]
    heads = width // HEAD_DIM
    return pl.pallas_call(
        functools.partial(attend_backward_kernel, heads, 512),
        out_shape=struct((3, width, length), BF),
        in_specs=whole(6),
        out_specs=pl.BlockSpec(memory_space=VM),
        scratch_shapes=[
            pltpu.VMEM((128, length), BF),
            pltpu.VMEM((128, length), BF),
            pltpu.VMEM((32, length), BF),
            pltpu.VMEM((32, length), BF),
            pltpu.VMEM((16, length), F32),
            pltpu.VMEM((16, length), F32),
        ],
        compiler_params=params(),
        cost_estimate=cost(heads * length * length * 2400, 6 * 2**20, heads * length * length),
        name="attend_backward",
    )(triple, patch, mine, other, mixed, logs)


def norm_rows(values):
    average = jnp.mean(values, axis=1, keepdims=True)
    scaling = lax.rsqrt(
        jnp.mean(values * values, axis=1, keepdims=True) - average * average + EPS
    )
    return (values - average) * scaling, scaling


def norm_rows_back(upstream, normed, scaling, gain):
    scaled = upstream * gain
    return scaling * (
        scaled
        - jnp.mean(scaled, axis=1, keepdims=True)
        - normed * jnp.mean(scaled * normed, axis=1, keepdims=True)
    )


def first_rows_kernel(
    me, part, near, far, features, weight, vectors, layer, middle, normed_cpe, scaling_cpe, residual, normed, scaling
):
    device = me[0]
    low = (
        part[...].astype(F32) + near[...].astype(F32) + far[...].astype(F32) + vectors[0:1, :]
    ).astype(BF)
    middle[...] = low
    width = features.shape[2]
    pre = vectors[1:2, :]
    for j in range(4):
        pre = pre + dot(low[:, j * width : (j + 1) * width], weight[j ^ device], NN)
    xhat, rate = norm_rows(pre)
    normed_cpe[...] = xhat
    scaling_cpe[...] = rate
    points = jnp.concatenate([features[j ^ device] for j in range(4)], axis=1)
    sums = points.astype(F32) + xhat * vectors[2:3, :] + vectors[3:4, :]
    residual[...] = sums
    xhat, rate = norm_rows(sums)
    normed[...] = xhat
    scaling[...] = rate
    layer[...] = (xhat * vectors[4:5, :] + vectors[5:6, :]).astype(BF)


def tiled(shape, tile, dim=0):
    block = list(shape)
    block[dim] = tile
    return pl.BlockSpec(tuple(block), lambda i: tuple(i if d == dim else 0 for d in range(len(shape))))


def fixed(shape):
    return pl.BlockSpec(shape, lambda i: (0,) * len(shape))


SMEM = pl.BlockSpec(memory_space=pltpu.SMEM)


def first_rows(me, part, near, far, features, weight, vectors):
    rows, wide = part.shape
    tile = 256
    outs = [
        struct((rows, wide), BF),
        struct((rows, wide), BF),
        struct((rows, wide), F32),
        struct((rows, 1), F32),
        struct((rows, wide), F32),
        struct((rows, wide), F32),
        struct((rows, 1), F32),
    ]
    return pl.pallas_call(
        first_rows_kernel,
        grid=(rows // tile,),
        out_shape=outs,
        in_specs=[
            SMEM,
            tiled(part.shape, tile),
            tiled(near.shape, tile),
            tiled(far.shape, tile),
            tiled(features.shape, tile, 1),
            fixed(weight.shape),
            fixed(vectors.shape),
        ],
        out_specs=[tiled(o.shape, tile) for o in outs],
        compiler_params=params(),
        cost_estimate=cost(6 * rows * wide * wide),
        name="first_rows",
    )(me, part, near, far, features, weight, vectors)


def gelu_parts(u):
    scale = math.sqrt(2 / math.pi)
    square = u * u
    bent = jnp.tanh(scale * u * (1.0 + 0.044715 * square))
    half = 0.5 * (1.0 + bent)
    slope = half + 0.5 * u * (1.0 - bent * bent) * (scale * (1.0 + 3 * 0.044715 * square))
    return u * half, slope


def second_rows_kernel(
    me, keep, got, residual, upstream, vectors, hidden_bias, w0, w1, w2, w3,
    block_out, active, before, layer, carried, low, grad_keep, grad_send, grad_hidden_bias, sums,
):
    device = me[0]
    packs = (w0, w1, w2, w3)
    wide = residual.shape[1]
    base = residual[...] + vectors[6:7, :]
    attended = (keep, got, keep, got)
    for e in range(4):
        spots = slice(e // 2 * 128, e // 2 * 128 + 128)
        base = base + dot(attended[e][spots, :], packs[e][2 * wide :, :], TN)
    normed, scaling = norm_rows(base)
    lower = (normed * vectors[7:8, :] + vectors[8:9, :]).astype(BF)
    layer[...] = lower
    grads = jnp.concatenate([upstream[j ^ device] for j in range(4)], axis=1)
    wide_grads = grads.astype(F32)
    result = base + vectors[9:10, :]
    grad_layer = jnp.zeros(residual.shape, F32)
    step = pl.program_id(0)

    def add(ref, index, value):
        @pl.when(step == 0)
        def _():
            ref[index, :] = value

        @pl.when(step != 0)
        def _():
            ref[index, :] = ref[index, :] + value

    for e in range(4):
        hidden, output = packs[e][0:wide, :], packs[e][wide : 2 * wide, :]
        act, slope = gelu_parts(dot(lower, hidden, NN) + hidden_bias[e : e + 1, :])
        act = act.astype(BF)
        active[e] = act
        result = result + dot(act, output, NN)
        pre = dot(grads, output, NT) * slope
        add(grad_hidden_bias, slice(e, e + 1), jnp.sum(pre, axis=0, keepdims=True))
        pre = pre.astype(BF)
        before[e] = pre
        grad_layer = grad_layer + dot(pre, hidden, NT)
    result = result.astype(BF)
    width = wide // 4
    for j in range(4):
        block_out[j ^ device] = result[:, j * width : (j + 1) * width]
    add(sums, slice(0, 1), jnp.sum(grad_layer * normed, axis=0, keepdims=True))
    add(sums, slice(1, 2), jnp.sum(grad_layer, axis=0, keepdims=True))
    add(sums, slice(3, 4), jnp.sum(wide_grads, axis=0, keepdims=True))
    carry = wide_grads + norm_rows_back(grad_layer, normed, scaling, vectors[7:8, :])
    carried[...] = carry
    add(sums, slice(2, 3), jnp.sum(carry, axis=0, keepdims=True))
    carry = carry.astype(BF)
    low[...] = carry
    for e in range(4):
        out = (grad_keep, grad_send, grad_keep, grad_send)[e]
        out[e // 2 * 128 : e // 2 * 128 + 128, :] = dot(packs[e][2 * wide :, :], carry, NT).astype(BF)


def second_rows(me, keep, got, residual, upstream, vectors, hidden_bias, packs):
    rows, wide = residual.shape
    tile = 256
    outs = [
        (struct((4, rows, wide // 4), BF), 1),
        (struct((4, rows, wide), BF), 1),
        (struct((4, rows, wide), BF), 1),
        (struct((rows, wide), BF), 0),
        (struct((rows, wide), F32), 0),
        (struct((rows, wide), BF), 0),
        (struct(keep.shape, BF), 1),
        (struct(keep.shape, BF), 1),
        (struct((4, wide), F32), None),
        (struct((4, wide), F32), None),
    ]
    return pl.pallas_call(
        second_rows_kernel,
        grid=(rows // tile,),
        out_shape=[o for o, dim in outs],
        in_specs=[
            SMEM,
            tiled(keep.shape, tile, 1),
            tiled(got.shape, tile, 1),
            tiled(residual.shape, tile),
            tiled(upstream.shape, tile, 1),
            fixed(vectors.shape),
            fixed(hidden_bias.shape),
        ]
        + [fixed(p.shape) for p in packs],
        out_specs=[fixed(o.shape) if dim is None else tiled(o.shape, tile, dim) for o, dim in outs],
        compiler_params=params(),
        cost_estimate=cost(36 * rows * wide * wide, 16 * 2**20),
        name="second_rows",
    )(me, keep, got, residual, upstream, vectors, hidden_bias, *packs)


def cut_rows(ref, index, cols, value, blocks):
    size = value.shape[0] // blocks
    for p in range(blocks):
        ref[index, p, :, cols] = value[p * size : (p + 1) * size].astype(ref.dtype)


def second_weights_kernel(blocks, which, upstream, active, before, layer, low, attended, out, wide_grads):
    wide = layer.shape[1]
    wide_grads[...] = upstream[...]
    for i, e in enumerate(which):
        cut_rows(out, i, slice(0, wide), dot(layer[...], before[e], TN), blocks)
        cut_rows(out, i, slice(wide, 2 * wide), dot(wide_grads[...], active[e], TN), blocks)
        part = dot(attended[i * 128 : (i + 1) * 128, :], low[...], NN)
        cut_rows(out, i, slice(2 * wide, 2 * wide + 128), part.T, blocks)


def second_weights(which, blocks, upstream, active, before, layer, low, attended):
    rows, wide = layer.shape
    return pl.pallas_call(
        functools.partial(second_weights_kernel, blocks, which),
        out_shape=struct((2, blocks, wide // blocks, 2 * wide + 128), BF),
        in_specs=whole(6),
        out_specs=pl.BlockSpec(memory_space=VM),
        scratch_shapes=[pltpu.VMEM((rows, wide), BF)],
        compiler_params=params(),
        cost_estimate=cost(9 * rows * wide * wide, 8 * 2**20),
        name="second_weights",
    )(upstream, active, before, layer, low, attended)


def triple_weights_kernel(blocks, grads, mine, other, out, sums):
    rows = mine.shape[0]
    width = grads.shape[1] // 2
    for t in range(3):
        for i in range(2):
            at = slice(i * width, (i + 1) * width)
            part = dot(grads[t, at, :rows], mine[...], NN) + dot(grads[t, at, rows:], other[...], NN)
            cut_rows(out, i, slice(t * width, (t + 1) * width), part.T, blocks)
        sums[t] = jnp.sum(grads[t].astype(F32), axis=1, keepdims=True)


def triple_weights(blocks, grads, mine, other):
    wide = mine.shape[1]
    width = grads.shape[1] // 2
    return pl.pallas_call(
        functools.partial(triple_weights_kernel, blocks),
        out_shape=(
            struct((2, blocks, wide // blocks, 3 * width), BF),
            struct((3, 2 * width, 1), F32),
        ),
        in_specs=whole(3),
        out_specs=whole(2),
        compiler_params=params(),
        cost_estimate=cost(12 * grads.shape[2] * wide * width),
        name="triple_weights",
    )(grads, mine, other)


def layer_grad_kernel(grads, weight, out):
    total = dot(grads[0], weight[0], TN) + dot(grads[1], weight[1], TN) + dot(grads[2], weight[2], TN)
    out[...] = total.astype(out.dtype)


def layer_grad(grads, weight, half, kind):
    width, length = grads.shape[1:]
    wide = weight.shape[1]
    rows = length // 2
    return pl.pallas_call(
        layer_grad_kernel,
        grid=(1,),
        out_shape=struct((rows, wide), kind),
        in_specs=[
            pl.BlockSpec((3, width, rows), lambda i: (0, 0, half)),
            fixed((3, width, wide)),
        ],
        out_specs=fixed((rows, wide)),
        compiler_params=params(),
        cost_estimate=cost(6 * rows * wide * width),
        name="layer_grad",
    )(grads, weight.reshape(3, width, wide))


def third_rows_kernel(
    me, part, near, carried, normed, scaling, normed_cpe, scaling_cpe, weight, vectors, conv_grad, points_grad, low, sums
):
    device = me[0]
    step = pl.program_id(0)

    def add(index, value):
        value = jnp.sum(value, axis=0, keepdims=True)

        @pl.when(step == 0)
        def _():
            sums[index, :] = value

        @pl.when(step != 0)
        def _():
            sums[index, :] = sums[index, :] + value

    upstream = part[...] + near[...].astype(F32)
    xhat = normed[...]
    add(slice(4, 5), upstream * xhat)
    add(slice(5, 6), upstream)
    grads = carried[...] + norm_rows_back(upstream, xhat, scaling[...], vectors[4:5, :])
    width = points_grad.shape[2]
    lower = grads.astype(BF)
    for j in range(4):
        points_grad[j ^ device] = lower[:, j * width : (j + 1) * width]
    xhat = normed_cpe[...]
    add(slice(2, 3), grads * xhat)
    add(slice(3, 4), grads)
    grads = norm_rows_back(grads, xhat, scaling_cpe[...], vectors[2:3, :])
    add(slice(1, 2), grads)
    lower = grads.astype(BF)
    low[...] = lower
    for j in range(4):
        at = slice(j * width, (j + 1) * width)
        piece = dot(lower, weight[j ^ device], NT)
        conv_grad[:, at] = piece.astype(BF)
        value = jnp.sum(piece, axis=0, keepdims=True)

        @pl.when(step == 0)
        def _():
            sums[0:1, at] = value

        @pl.when(step != 0)
        def _():
            sums[0:1, at] = sums[0:1, at] + value


def third_rows(me, part, near, carried, normed, scaling, normed_cpe, scaling_cpe, weight, vectors):
    rows, wide = part.shape
    tile = 256
    outs = [
        (struct((rows, wide), BF), 0),
        (struct((4, rows, wide // 4), BF), 1),
        (struct((rows, wide), BF), 0),
        (struct((6, wide), F32), None),
    ]
    return pl.pallas_call(
        third_rows_kernel,
        grid=(rows // tile,),
        out_shape=[o for o, dim in outs],
        in_specs=[SMEM]
        + [tiled(a.shape, tile) for a in (part, near, carried, normed, scaling, normed_cpe, scaling_cpe)]
        + [fixed(weight.shape), fixed(vectors.shape)],
        out_specs=[fixed(o.shape) if dim is None else tiled(o.shape, tile, dim) for o, dim in outs],
        compiler_params=params(),
        cost_estimate=cost(6 * rows * wide * wide),
        name="third_rows",
    )(me, part, near, carried, normed, scaling, normed_cpe, scaling_cpe, weight, vectors)


def cpe_weights_kernel(blocks, me, middle, low, out):
    device = me[0]
    for e in range(4):
        at = pl.ds(pl.multiple_of((e ^ device) * 128, 128), 128)
        cut_rows(out, e, slice(0, 128), dot(low[...], middle[:, at], TN), blocks)


def cpe_weights(blocks, me, middle, low):
    rows, wide = middle.shape
    return pl.pallas_call(
        functools.partial(cpe_weights_kernel, blocks),
        out_shape=struct((4, blocks, wide // blocks, 128), BF),
        in_specs=[SMEM] + whole(2),
        out_specs=pl.BlockSpec(memory_space=VM),
        compiler_params=params(),
        cost_estimate=cost(2 * rows * wide * wide),
        name="cpe_weights",
    )(me, middle, low)


def swap(values, e, axis="blk"):
    return lax.ppermute(values, axis, [(i, i ^ e) for i in range(lax.axis_size(axis))])


def pick(values, index):
    return lax.dynamic_index_in_dim(values, index, 0, keepdims=False)


def in_order(pieces, me):
    core, chip = (me & 1) == 1, (me >> 1) == 1
    a, b = jnp.where(core, pieces[1], pieces[0]), jnp.where(core, pieces[0], pieces[1])
    c, d = jnp.where(core, pieces[3], pieces[2]), jnp.where(core, pieces[2], pieces[3])
    return [
        jnp.where(chip, c, a),
        jnp.where(chip, d, b),
        jnp.where(chip, a, c),
        jnp.where(chip, b, d),
    ]


def scatter_sum(values, spot):
    count = values.shape[0]
    if count & (count - 1):
        return lax.psum_scatter(values, "pts", scatter_dimension=0, tiled=False).astype(F32)
    stage = 0
    while count > 1:
        values = values.reshape(count // 2, 2, *values.shape[1:])
        bit = (spot >> stage) & 1
        mine = lax.dynamic_index_in_dim(values, bit, 1, keepdims=False)
        theirs = lax.dynamic_index_in_dim(values, 1 - bit, 1, keepdims=False)
        count //= 2
        values = mine.astype(F32) + swap(theirs, 1 << stage, "pts").astype(F32)
        if count > 1:
            values = values.astype(BF)
        stage += 1
    return values[0]


def all_sum(values):
    count = lax.axis_size("pts")
    if count & (count - 1):
        return lax.psum(values, "pts")
    stage = 1
    while stage < count:
        values = values + swap(values, stage, "pts")
        stage *= 2
    return values


def shards(
    points, neighbours, patch_ids, conv_weight, conv_bias, cpe_weight, cpe_bias, cpe_gain, cpe_shift, first_gain,
    first_shift, qkv_weight, query_value_bias, proj_weight, proj_bias, second_gain, second_shift, hidden_weight,
    hidden_bias, output_weight, output_bias, out_grad,
):
    row_count, width = points.shape
    wide = conv_weight.shape[2]
    mine = row_count // 4
    shard_count = lax.axis_size("pts")
    me = lax.axis_index("blk")
    spot = lax.axis_index("pts")
    me_ref = me.astype(jnp.int32).reshape(1)
    ups = [(i, i + 1) for i in range(shard_count - 1)]
    downs = [(i + 1, i) for i in range(shard_count - 1)]

    low = lax.ppermute(points[row_count - REACH :], "pts", ups)
    high = lax.ppermute(points[:REACH], "pts", downs)
    padded = jnp.concatenate([low, points, high], axis=0)
    lookup = (neighbours - spot * row_count + REACH).T
    lookup = jnp.concatenate([lookup, jnp.zeros((5, row_count), jnp.int32)], axis=0)

    def quarter(values, e, dim=0, extra=0):
        return lax.dynamic_slice_in_dim(values, (me ^ e) * mine, mine + extra, dim)

    windows = [quarter(padded, e, 0, 2 * REACH) for e in range(4)]
    places = [quarter(lookup, e, 1) - (me ^ e) * mine for e in range(4)]
    kernel_rows = conv_weight.reshape(KERNEL * width, wide)

    def exchange(values):
        return [quarter(values, 0)] + [swap(quarter(values, e), e) for e in (1, 2, 3)]

    def collect(values):
        first = swap(values, 1)
        second = swap(values, 2)
        return [values, first, second, swap(second, 1)]

    small = jnp.stack(
        [conv_bias, cpe_bias, cpe_gain, cpe_shift, first_gain, first_shift, proj_bias, second_gain, second_shift, output_bias]
    )
    small = jnp.concatenate([small, hidden_bias.reshape(4, width), query_value_bias], axis=0)
    small = collect(small)
    vectors = jnp.concatenate([s for s in in_order(small, me)], axis=1)
    hidden_biases = jnp.stack([s[10:14].reshape(4 * width) for s in small])
    cpe_pieces = jnp.stack(collect(cpe_weight))
    features = jnp.stack(exchange(points))
    turned = qkv_weight.transpose(1, 2, 0)
    other_turned = swap(turned, 2)
    head_weight = jnp.concatenate([turned, other_turned], axis=1).reshape(6 * width, wide)
    head_bias = jnp.stack(
        [
            jnp.concatenate([small[0][14], small[2][14]]),
            jnp.zeros((2 * width,), F32),
            jnp.concatenate([small[0][15], small[2][15]]),
        ]
    ).reshape(6 * width, 1)

    part3, gathered3 = conv_forward(windows[3], places[3], kernel_rows, BF)
    got3 = swap(part3, 1)
    part2, gathered2 = conv_forward(windows[2], places[2], kernel_rows, BF)
    far = swap((part2.astype(F32) + got3.astype(F32)).astype(BF), 2)
    part1, gathered1 = conv_forward(windows[1], places[1], kernel_rows, BF)
    near = swap(part1, 1)
    part0, gathered0 = conv_forward(windows[0], places[0], kernel_rows, F32)

    layer_one, conv_low, normed_cpe, scaling_cpe, residual_one, normed_one, scaling_one = first_rows(
        me_ref, part0, near, far, features, cpe_pieces, vectors
    )
    other_one = swap(layer_one, 1)
    patch_row = jnp.concatenate([quarter(patch_ids, 0), quarter(patch_ids, 1)]).reshape(1, 2 * mine)

    packs = collect(jnp.concatenate([hidden_weight, output_weight, proj_weight], axis=0))
    upstream = jnp.stack(exchange(out_grad))

    triple, mixed, keep, send, logs = attend_forward(layer_one, other_one, head_weight, head_bias, patch_row)
    got = swap(send, 1)
    (
        block_pieces, active, before, layer_two, carried, carried_low, grad_keep, grad_send, sum_hidden_bias, sums_two,
    ) = second_rows(me_ref, keep, got, residual_one, upstream, vectors, hidden_biases, packs)
    grad_got = swap(grad_send, 1)

    grads_wide = jnp.concatenate(in_order(upstream, me), axis=1)
    weights_send = second_weights((1, 3), shard_count, grads_wide, active, before, layer_two, carried_low, got)
    weights_got = swap(weights_send, 1)
    weights_keep = second_weights((0, 2), shard_count, grads_wide, active, before, layer_two, carried_low, keep)
    weights_sum = (weights_keep.astype(F32) + weights_got.astype(F32)).astype(BF)
    weights_far = swap(weights_sum[1], 2)
    second_sum = (weights_sum[0].astype(F32) + weights_far.astype(F32)).astype(BF)

    grad_triple = attend_backward(triple, patch_row, grad_keep, grad_got, mixed, logs)
    layer_send = layer_grad(grad_triple, head_weight, 1, BF)
    layer_got = swap(layer_send, 1)
    layer_part = layer_grad(grad_triple, head_weight, 0, F32)
    conv_grad, points_pieces, cpe_low, sums_one = third_rows(
        me_ref, layer_part, layer_got, carried, normed_one, scaling_one, normed_cpe, scaling_cpe, cpe_pieces, vectors
    )

    grad0 = conv_grad
    grad1 = swap(grad0, 1)
    grad2 = swap(grad0, 2)
    grad3 = swap(grad2, 1)
    spread0 = spread(places[0], kernel_rows, grad0)
    spread1 = spread(places[1], kernel_rows, grad1)

    triple_grads, triple_sums = triple_weights(shard_count, grad_triple, layer_one, other_one)
    cpe_grads = cpe_weights(shard_count, me_ref, conv_low, cpe_low)
    cpe_got = swap(jnp.stack([cpe_grads[1], cpe_grads[3]]), 1)
    cpe_keep = (jnp.stack([cpe_grads[0], cpe_grads[2]]).astype(F32) + cpe_got.astype(F32)).astype(BF)
    third_grads = jnp.concatenate([triple_grads, cpe_keep], axis=3)
    third_sum = (third_grads[0].astype(F32) + swap(third_grads[1], 2).astype(F32)).astype(BF)

    gathered = (gathered0, gathered1, gathered2, gathered3)
    grads = (grad0, grad1, grad2, grad3)
    cuts = 3
    chunk = KERNEL // cuts * width
    conv_sums = []
    for i in range(cuts):
        piece = conv_weight_grad(gathered, grads, i * chunk, chunk, shard_count)
        conv_sums.append(scatter_sum(piece, spot))
    spread2 = spread(places[2], kernel_rows, grad2)
    spread3 = spread(places[3], kernel_rows, grad3)

    second_sum = scatter_sum(second_sum, spot)
    third_sum = scatter_sum(third_sum, spot)

    sums = jnp.concatenate([sums_one, sums_two], axis=0)
    width_pieces = [sums[:, j * width : (j + 1) * width] for j in range(4)]
    width_pieces = in_order(width_pieces, me)
    triple_sums = triple_sums[:, :, 0]
    empty = jnp.zeros((2, width), F32)
    heads_pieces = [
        jnp.stack([triple_sums[0, :width], triple_sums[2, :width]]),
        empty,
        jnp.stack([triple_sums[0, width:], triple_sums[2, width:]]),
        empty,
    ]
    small = jnp.stack(
        [
            jnp.concatenate([width_pieces[e], sum_hidden_bias[e].reshape(4, width), heads_pieces[e]], axis=0)
            for e in range(4)
        ]
    )
    small = jnp.stack([small[0], small[2]]) + swap(jnp.stack([small[1], small[3]]), 1)
    small = all_sum(small[0] + swap(small[1], 2))

    spreads = in_order([spread0, spread1, spread2, spread3], me)
    grad_padded = jnp.zeros((width, row_count + 2 * REACH), F32)
    for q in range(4):
        grad_padded = grad_padded + jnp.pad(spreads[q], ((0, 0), (q * mine, (3 - q) * mine)))
    from_above = lax.ppermute(grad_padded[:, :REACH].astype(BF), "pts", downs).astype(F32)
    from_below = lax.ppermute(grad_padded[:, row_count + REACH :].astype(BF), "pts", ups).astype(F32)
    inside = grad_padded[:, REACH : REACH + row_count]
    inside = inside + jnp.pad(from_below, ((0, 0), (0, row_count - REACH)))
    inside = inside + jnp.pad(from_above, ((0, 0), (row_count - REACH, 0)))
    points_rows = [points_pieces[0]] + [swap(points_pieces[e], e) for e in (1, 2, 3)]
    points_rows = jnp.concatenate(in_order(points_rows, me), axis=0)
    grad_points = points_rows.astype(F32) + inside.T
    block_rows = [block_pieces[0]] + [swap(block_pieces[e], e) for e in (1, 2, 3)]
    block_out = jnp.concatenate(in_order(block_rows, me), axis=0)

    cols = wide // shard_count
    grad_conv = jnp.concatenate(conv_sums, axis=1).T.reshape(KERNEL, width, cols)
    return (
        block_out,
        grad_points,
        grad_conv,
        small[0],
        third_sum[:, 3 * width :].T,
        small[1],
        small[2],
        small[3],
        small[4],
        small[5],
        third_sum[:, : 3 * width].reshape(cols, 3, width),
        small[14:16],
        second_sum[:, 2 * wide :].T,
        small[8],
        small[6],
        small[7],
        second_sum[:, :wide],
        small[10:14].reshape(4 * width),
        second_sum[:, wide : 2 * wide].T,
        small[9],
    )


def solution(mesh):
    return jax.shard_map(
        shards,
        mesh=mesh,
        in_specs=(
            P("pts", "blk"),
            P("pts", None),
            P("pts"),
            P(None, "blk", None),
            P("blk"),
            P("blk", None),
            P("blk"),
            P("blk"),
            P("blk"),
            P("blk"),
            P("blk"),
            P(None, None, "blk"),
            P(None, "blk"),
            P("blk", None),
            P("blk"),
            P("blk"),
            P("blk"),
            P(None, "blk"),
            P("blk"),
            P("blk", None),
            P("blk"),
            P("pts", "blk"),
        ),
        out_specs=(
            P("pts", "blk"),
            P("pts", "blk"),
            P(None, "blk", "pts"),
            P("blk"),
            P("blk", "pts"),
            P("blk"),
            P("blk"),
            P("blk"),
            P("blk"),
            P("blk"),
            P("pts", None, "blk"),
            P(None, "blk"),
            P("blk", "pts"),
            P("blk"),
            P("blk"),
            P("blk"),
            P("pts", "blk"),
            P("blk"),
            P("blk", "pts"),
            P("blk"),
        ),
        check_vma=False,
    )
```

time: 1620 us -> 399 us (0.25)
  the two profiles are of different devices: /device:TPU:5 before, /device:TPU:0 now
where the time goes in v1:
time: 399 us; the launch traced here: 394 us
  Pallas kernels  180 us (45%)
  waiting for transfers between devices  86.8 us (22%)
  starting transfers between devices  53.2 us (13%)
  local copies, waits for them, and re-layouts  48.6 us (12%)
  other arithmetic  24.3 us (6%)
    ppermute x56, waiting for transfers between devices, swap(): lax.ppermute(values, axis, [(i, i ^ e) for i in range(lax.axis_size(axis))])  82.6 us
    ppermute x56, starting transfers between devices, swap(): lax.ppermute(values, axis, [(i, i ^ e) for i in range(lax.axis_size(axis))])  43.1 us
    pallas_call x1, Pallas kernels, attend_backward(): pl.pallas_call(functools.partial(attend_backward_kernel, heads, 512), out...  38.3 us
    pallas_call x4, Pallas kernels, conv_forward(): pl.pallas_call(conv_kernel, out_shape=(struct((rows, wide), kind), struct...  30.2 us
    unnamed x138, local copies, waits for them, and re-layouts  29.7 us
    pallas_call x4, Pallas kernels, spread(): pl.pallas_call(spread_kernel, out_shape=struct((width, rows + 2 * REACH),...  27.1 us
    pallas_call x1, Pallas kernels, attend_forward(): pl.pallas_call(functools.partial(attend_forward_kernel, heads, 512), out_...  21.2 us
    pallas_call x3, Pallas kernels, conv_weight_grad(): pl.pallas_call(functools.partial(conv_weight_kernel, blocks), grid=(count...  18.4 us
  transfers between devices with their start and end apart: 60, of which 21 were waited for; matrix products, arithmetic and copies ran while one was open for 11% of the time, Pallas kernels for 41%

profile of v1, /device:TPU:0, one launch (start us, length us, event | category | flops | bytes accessed | tf_op | source)
XLA Modules:
  0.0 394.5 jit_solution(17399275333716304426)
XLA Ops:
  2.3 3.0 collective-permute-start.11
  7.3 4.3 %collective-permute-start = (bf16[256,128]{1,0:T(8,128)(2,1)}, bf16[256,128]{1,0:T(8,128)(2,1)}, u32[]{:S(2)}, u32[]{:S(2)}) collective-permute-start(bf16[256,128]{1,0:T(8,128)(2,1)} %get-tuple-element.180), channel_id=1, source_target_pairs={{0,4},{4,8},{8,12},{12,16},{16,20},{20,24},{24,28},{1,5},{5,9},{9,... | collective-permute-start | bytes 196616 | tf_op jit(solution)/shard_map/ppermute | solution.py:769
  21.5 2.2 collective-permute-done.1
  23.9 7.5 %conv_forward.7 = (bf16[512,512]{1,0:T(8,128)(2,1)S(1)}, bf16[3456,512]{1,0:T(8,128)(2,1)S(1)}) custom-call(bf16[1024,128]{1,0:T(8,128)(2,1)S(1)} %get-tuple-element.158.window, s32[32,512]{1,0:T(8,128)S(1)} %get-tuple-element.185.place, bf16[3456,512]{1,0:T(8,128)(2,1)} %bitcast.255), custom_call_target="tpu_custom_call" | custom-call | flops 3623878656 | bytes 4194304 | tf_op jit(solution)/shard_map/conv_forward/pallas_call | solution.py:72
  31.4 1.8 copy-done
  33.2 7.5 %conv_forward.6 = (bf16[512,512]{1,0:T(8,128)(2,1)S(1)}, bf16[3456,512]{1,0:T(8,128)(2,1)S(1)}) custom-call(bf16[1024,128]{1,0:T(8,128)(2,1)S(1)} %get-tuple-element.157.window, s32[32,512]{1,0:T(8,128)S(1)} %get-tuple-element.183.place, bf16[3456,512]{1,0:T(8,128)(2,1)} %bitcast.256), custom_call_target="tpu_custom_call" | custom-call | flops 3623878656 | bytes 4194304 | tf_op jit(solution)/shard_map/conv_forward/pallas_call | solution.py:72
  40.6 1.8 copy-done.1
  42.5 7.8 %conv_forward.5 = (bf16[512,512]{1,0:T(8,128)(2,1)S(1)}, bf16[3456,512]{1,0:T(8,128)(2,1)S(1)}) custom-call(bf16[1024,128]{1,0:T(8,128)(2,1)S(1)} %get-tuple-element.159.window, s32[32,512]{1,0:T(8,128)S(1)} %get-tuple-element.184.place, bf16[3456,512]{1,0:T(8,128)(2,1)} %bitcast.257), custom_call_target="tpu_custom_call" | custom-call | flops 3623878656 | bytes 4194304 | tf_op jit(solution)/shard_map/conv_forward/pallas_call | solution.py:72
  50.2 1.8 copy-done.2
  55.0 2.6 collective-permute-done.7
  58.7 7.5 %conv_forward.4 = (f32[512,512]{1,0:T(8,128)S(1)}, bf16[3456,512]{1,0:T(8,128)(2,1)S(1)}) custom-call(bf16[1024,128]{1,0:T(8,128)(2,1)S(1)} %get-tuple-element.160.window, s32[32,512]{1,0:T(8,128)S(1)} %get-tuple-element.186.place, bf16[3456,512]{1,0:T(8,128)(2,1)} %bitcast.258), custom_call_target="tpu_custom_call" | custom-call | flops 3623878656 | bytes 4194304 | tf_op jit(solution)/shard_map/conv_forward/pallas_call | solution.py:72
  70.7 24.4 %collective-permute-done.4.far = bf16[512,512]{1,0:T(8,128)(2,1)S(1)} collective-permute-done((bf16[512,512]{1,0:T(8,128)(2,1)S(1)}, bf16[512,512]{1,0:T(8,128)(2,1)S(1)}, u32[]{:S(2)}, u32[]{:S(2)}) %collective-permute-start.4) | collective-permute-done | bytes 524320 | tf_op jit(solution)/shard_map/ppermute | solution.py:706
  95.0 14.7 %first_rows.1 = (bf16[512,512]{1,0:T(8,128)(2,1)S(1)}, bf16[512,512]{1,0:T(8,128)(2,1)S(1)}, f32[512,512]{1,0:T(8,128)S(1)}, f32[512,1]{1,0:T(8,128)S(1)}, f32[5...) custom-call(s32[1]{0:T(128)} %bitcast.me, f32[512,512]{1,0:T(8,128)} %copy-done.14, ...), custom_call_target="tpu_custom_call" | custom-call | flops 805306368 | bytes 4194304 | tf_op jit(solution)/shard_map/first_rows/pallas_call | solution.py:409
  117.7 21.2 %attend_forward.1 = (bf16[3,256,1024]{2,1,0:T(8,128)(2,1)S(1)}, f32[256,1024]{1,0:T(8,128)S(1)}, bf16[256,512]{1,0:T(8,128)(2,1)S(1)}, bf16[256,512]{1,0:T(8,128)(2,1)S(1)}, f32[16,1024]{1,0:T(8,128)S(1)}) custom-call(bf16[512,512]{1,0:T(8,128)(2,1)S(1)} %get-tuple-element.60.mine, bf16[512,512]{1,0:T(8,128)(2,1)S(1)} %collective-permute-done.14.other, ...), custom_call_target="tpu_custom_call" | custom-call | flops 20132659200 | bytes 6291456 | tf_op jit(solution)/shard_map/attend_forward/pallas_call | solution.py:257
  142.6 14.3 %second_rows.1 = (bf16[4,512,128]{2,1,0:T(8,128)(2,1)S(1)}, bf16[4,512,512]{2,1,0:T(8,128)(2,1)}, bf16[4,512,512]{2,1,0:T(8,128)(2,1)}, bf16[512,512]{1,0:T(8,12...) custom-call(s32[1]{0:T(128)} %bitcast.me, ...), custom_call_target="tpu_custom_call" | custom-call | flops 4831838208 | bytes 16777216 | tf_op jit(solution)/shard_map/second_rows/pallas_call | solution.py:511
  156.9 2.0 copy-done.4
  160.4 2.9 second_weights.3
  165.8 2.9 second_weights.2
  169.3 3.2 collective-permute-done.24
  172.6 38.3 %attend_backward.1.grads = bf16[3,256,1024]{2,1,0:T(8,128)(2,1)S(1)} custom-call(bf16[3,256,1024]{2,1,0:T(8,128)(2,1)S(1)} %get-tuple-element.65.triple, s32[1,1024]{1,0:T(1,128)S(1)} %bitcast.254, bf16[256,512]{1,0:T(8,128)(2,1)S(1)} %get-tuple-element.66.mine, bf16[256,512]{1,0:T(8,128)(2,1)S(1)} %collective-permute-done.26.other, ...), custom_call_target="tpu_custom_call" | custom-call | flops 40265318400 | bytes 6291456 | tf_op jit(solution)/shard_map/attend_backward/pallas_call | solution.py:324
  219.6 5.8 %third_rows.1 = (bf16[512,512]{1,0:T(8,128)(2,1)S(1)}, bf16[4,512,128]{2,1,0:T(8,128)(2,1)S(1)}, bf16[512,512]{1,0:T(8,128)(2,1)S(1)}, f32[6,512]{1,0:T(8,128)S(1)}) custom-call(s32[1]{0:T(128)} %bitcast.me, f32[512,512]{1,0:T(8,128)S(1)} %layer_grad.2.part, bf16[512,512]{1,0:T(8,128)(2,1)S(1)} %copy-done.19, f32[512,512]{1,0:T(8,128)S(1)} %copy-done.17, ...), custom_call_target="tpu_custom_call" | custom-call | flops 805306368 | bytes 4194304 | tf_op jit(solution)/shard_map/third_rows/pallas_call | solution.py:671
  226.9 6.8 %spread.7 = f32[128,1024]{1,0:T(8,128)S(1)} custom-call(s32[32,512]{1,0:T(8,128)S(1)} %copy-done.33, bf16[3456,512]{1,0:T(8,128)(2,1)S(1)} %bitcast.259, bf16[512,512]{1,0:T(8,128)(2,1)S(1)} %get-tuple-element.76.grads.refs_4_), custom_call_target="tpu_custom_call" | custom-call | flops 3623878656 | bytes 4194304 | tf_op jit(solution)/shard_map/spread/pallas_call | solution.py:112
  236.4 3.6 collective-permute-done.46
  240.0 1.8 collective-permute-start.47
  247.3 2.4 collective-permute-start.49
  261.6 2.0 copy-done.35
  263.6 6.9 %spread.5 = f32[128,1024]{1,0:T(8,128)S(1)} custom-call(s32[32,512]{1,0:T(8,128)S(1)} %copy-done.31, bf16[3456,512]{1,0:T(8,128)(2,1)S(1)} %bitcast.260, bf16[512,512]{1,0:T(8,128)(2,1)S(1)} %collective-permute-done.31.grads.refs_6_), custom_call_target="tpu_custom_call" | custom-call | flops 3623878656 | bytes 4194304 | tf_op jit(solution)/shard_map/spread/pallas_call | solution.py:112
  271.4 2.0 collective-permute-done.51
  274.7 2.1 collective-permute-start.52
  276.8 2.0 copy-done.36
  278.8 6.7 %spread.6 = f32[128,1024]{1,0:T(8,128)S(1)} custom-call(s32[32,512]{1,0:T(8,128)S(1)} %copy-done.29, bf16[3456,512]{1,0:T(8,128)(2,1)S(1)} %bitcast.261, bf16[512,512]{1,0:T(8,128)(2,1)S(1)} %collective-permute-done.33.grads.refs_5_), custom_call_target="tpu_custom_call" | custom-call | flops 3623878656 | bytes 4194304 | tf_op jit(solution)/shard_map/spread/pallas_call | solution.py:112
  288.5 6.1 %conv_weight_grad.3 = bf16[8,64,1152]{2,1,0:T(8,128)(2,1)S(1)} custom-call(bf16[3456,512]{1,0:T(8,128)(2,1)} %copy-done.3, bf16[3456,512]{1,0:T(8,128)(2,1)} %copy-done.2, bf16[3456,512]{1,0:T(8,128)(2,1)} %copy-done.1, bf16[3456,512]{1,0:T(8,128)(2,1)} %copy-done, bf16[512,512]{1,0:T(8,128)(2,1)S(1)} %get-tuple-element.76.grads.refs_4_, ...), custom_call_target="tpu_custom_call" | custom-call | flops 2415919104 | bytes 4194304 | tf_op jit(solution)/shard_map/conv_weight_grad/pallas_call | solution.py:143
  296.6 6.3 %conv_weight_grad.4 = bf16[8,64,1152]{2,1,0:T(8,128)(2,1)S(1)} custom-call(bf16[3456,512]{1,0:T(8,128)(2,1)} %copy-done.3, bf16[3456,512]{1,0:T(8,128)(2,1)} %copy-done.2, bf16[3456,512]{1,0:T(8,128)(2,1)} %copy-done.1, bf16[3456,512]{1,0:T(8,128)(2,1)} %copy-done, bf16[512,512]{1,0:T(8,128)(2,1)S(1)} %get-tuple-element.76.grads.refs_4_, ...), custom_call_target="tpu_custom_call" | custom-call | flops 2415919104 | bytes 4194304 | tf_op jit(solution)/shard_map/conv_weight_grad/pallas_call | solution.py:143
  304.8 6.7 %spread.4 = f32[128,1024]{1,0:T(8,128)S(1)} custom-call(s32[32,512]{1,0:T(8,128)S(1)} %get-tuple-element.185.place, bf16[3456,512]{1,0:T(8,128)(2,1)S(1)} %bitcast.262, bf16[512,512]{1,0:T(8,128)(2,1)S(1)} %copy-done.10), custom_call_target="tpu_custom_call" | custom-call | flops 3623878656 | bytes 4194304 | tf_op jit(solution)/shard_map/spread/pallas_call | solution.py:112
  312.3 2.0 copy.69
  316.2 3.1 collective-permute-start.34
  319.3 6.0 %conv_weight_grad.5 = bf16[8,64,1152]{2,1,0:T(8,128)(2,1)S(1)} custom-call(bf16[3456,512]{1,0:T(8,128)(2,1)} %copy-done.3, bf16[3456,512]{1,0:T(8,128)(2,1)} %copy-done.2, bf16[3456,512]{1,0:T(8,128)(2,1)} %copy-done.1, bf16[3456,512]{1,0:T(8,128)(2,1)} %copy-done, bf16[512,512]{1,0:T(8,128)(2,1)S(1)} %get-tuple-element.76.grads.refs_4_, ...), custom_call_target="tpu_custom_call" | custom-call | flops 2415919104 | bytes 4194304 | tf_op jit(solution)/shard_map/conv_weight_grad/pallas_call | solution.py:143
  327.8 3.0 collective-permute-start.42
  330.8 1.9 collective-permute-done.35
  335.2 2.7 collective-permute-done.54
  339.2 2.4 add_convert_fusion
  348.3 9.1 %collective-permute-done.37 = bf16[2,64,1152]{2,1,0:T(8,128)(2,1)S(1)} collective-permute-done((bf16[2,64,1152]{2,1,0:T(8,128)(2,1)S(1)}, bf16[2,64,1152]{2,1,0:T(8,128)(2,1)S(1)}, u32[]{:S(2)}, u32[]{:S(2)}) %collective-permute-start.37) | collective-permute-done | bytes 294944 | tf_op jit(solution)/shard_map/ppermute | solution.py:706
  357.6 3.5 collective-permute-done.40
  361.4 4.4 %collective-permute-done.43 = bf16[2,64,1152]{2,1,0:T(8,128)(2,1)S(1)} collective-permute-done((bf16[2,64,1152]{2,1,0:T(8,128)(2,1)S(1)}, bf16[2,64,1152]{2,1,0:T(8,128)(2,1)S(1)}, u32[]{:S(2)}, u32[]{:S(2)}) %collective-permute-start.43) | collective-permute-done | bytes 294944 | tf_op jit(solution)/shard_map/ppermute | solution.py:706
  366.3 2.2 collective-permute-start.57
  369.6 7.4 %collective-permute-done.57 = bf16[4,64,1152]{2,1,0:T(8,128)(2,1)S(1)} collective-permute-done((bf16[4,64,1152]{2,1,0:T(8,128)(2,1)S(1)}, bf16[4,64,1152]{2,1,0:T(8,128)(2,1)S(1)}, u32[]{:S(2)}, u32[]{:S(2)}) %collective-permute-start.57) | collective-permute-done | bytes 589856 | tf_op jit(solution)/shard_map/ppermute | solution.py:706
  377.4 8.2 %collective-permute-done.58 = bf16[2,64,1152]{2,1,0:T(8,128)(2,1)S(1)} collective-permute-done((bf16[2,64,1152]{2,1,0:T(8,128)(2,1)S(1)}, bf16[2,64,1152]{2,1,0:T(8,128)(2,1)S(1)}, u32[]{:S(2)}, u32[]{:S(2)}) %collective-permute-start.58) | collective-permute-done | bytes 294944 | tf_op jit(solution)/shard_map/ppermute | solution.py:706
  387.5 5.3 %collective-permute-done.59 = bf16[1,64,1152]{2,1,0:T(8,128)(2,1)S(1)} collective-permute-done((bf16[1,64,1152]{2,1,0:T(8,128)(2,1)S(1)}, bf16[1,64,1152]{2,1,0:T(8,128)(2,1)S(1)}, u32[]{:S(2)}, u32[]{:S(2)}) %collective-permute-start.59) | collective-permute-done | bytes 147488 | tf_op jit(solution)/shard_map/ppermute | solution.py:706
  (336 shorter events, 98.5 us)
Async XLA Ops:
  2.3 14.9 %collective-permute-start.11 = (f32[16,128]{1,0:T(8,128)S(1)}, f32[16,128]{1,0:T(8,128)S(1)}, u32[]{:S(2)}, u32[]{:S(2)}) collective-permute-start(f32[16,128]{1,0:T(8,128)S(1)} %concatenate.59), channel_id=1, source_target_pairs={{0,2},{1,3},{2,0},{3,1},{4,6},{5,7},{6,4},{7,5},{8,10},{9,11},{10,... | collective-permute-start | bytes 24584 | tf_op jit(solution)/shard_map/ppermute | solution.py:706
  5.3 11.9 %collective-permute-start.13 = (f32[16,128]{1,0:T(8,128)S(1)}, f32[16,128]{1,0:T(8,128)S(1)}, u32[]{:S(2)}, u32[]{:S(2)}) collective-permute-start(f32[16,128]{1,0:T(8,128)S(1)} %concatenate.59), channel_id=1, source_target_pairs={{0,1},{1,0},{2,3},{3,2},{4,5},{5,4},{6,7},{7,6},{8,9},{9,8},{10,11... | collective-permute-start | bytes 24584 | tf_op jit(solution)/shard_map/ppermute | solution.py:706
  5.3 49.2 %collective-permute-start.9 = (bf16[128,512]{1,0:T(8,128)(2,1)}, bf16[128,512]{1,0:T(8,128)(2,1)S(1)}, u32[]{:S(2)}, u32[]{:S(2)}) collective-permute-start(bf16[128,512]{1,0:T(8,128)(2,1)} %param.27), channel_id=1, source_target_pairs={{0,2},{1,3},{2,0},{3,1},{4,6},{5,7},{6,4},{7,5},{8,10},{9,11},{10,... | collective-permute-start | bytes 393224 | tf_op jit(solution)/shard_map/ppermute | solution.py:706
  5.4 63.6 %collective-permute-start.8 = (bf16[128,512]{1,0:T(8,128)(2,1)}, bf16[128,512]{1,0:T(8,128)(2,1)S(1)}, u32[]{:S(2)}, u32[]{:S(2)}) collective-permute-start(bf16[128,512]{1,0:T(8,128)(2,1)} %param.27), channel_id=1, source_target_pairs={{0,1},{1,0},{2,3},{3,2},{4,5},{5,4},{6,7},{7,6},{8,9},{9,8},{10,11... | collective-permute-start | bytes 393224 | tf_op jit(solution)/shard_map/ppermute | solution.py:706
  7.3 11.7 %collective-permute-start = (bf16[256,128]{1,0:T(8,128)(2,1)}, bf16[256,128]{1,0:T(8,128)(2,1)}, u32[]{:S(2)}, u32[]{:S(2)}) collective-permute-start(bf16[256,128]{1,0:T(8,128)(2,1)} %get-tuple-element.180), channel_id=1, source_target_pairs={{0,4},{4,8},{8,12},{12,16},{16,20},{20,24},{24,28},{1,5},{5,9},{9,... | collective-permute-start | bytes 196616 | tf_op jit(solution)/shard_map/ppermute | solution.py:769
  17.2 6.6 %collective-permute-start.1 = (bf16[256,128]{1,0:T(8,128)(2,1)}, bf16[256,128]{1,0:T(8,128)(2,1)S(1)}, u32[]{:S(2)}, u32[]{:S(2)}) collective-permute-start(bf16[256,128]{1,0:T(8,128)(2,1)} %get-tuple-element.179), channel_id=1, source_target_pairs={{4,0},{8,4},{12,8},{16,12},{20,16},{24,20},{28,24},{5,1},{9,5},{13... | collective-permute-start | bytes 196616 | tf_op jit(solution)/shard_map/ppermute | solution.py:770
  18.5 35.3 %collective-permute-start.5 = (bf16[512,128]{1,0:T(8,128)(2,1)S(1)}, bf16[512,128]{1,0:T(8,128)(2,1)S(1)}, u32[]{:S(2)}, u32[]{:S(2)}) collective-permute-start(bf16[512,128]{1,0:T(8,128)(2,1)S(1)} %get-tuple-element.176), channel_id=1, source_target_pairs={{0,1},{1,0},{2,3},{3,2},{4,5},{5,4},{6,7},{7,6},{8,9},{9,8},{10,11... | collective-permute-start | bytes 393224 | tf_op jit(solution)/shard_map/ppermute | solution.py:706
  19.1 35.4 %collective-permute-start.6 = (bf16[512,128]{1,0:T(8,128)(2,1)S(1)}, bf16[512,128]{1,0:T(8,128)(2,1)S(1)}, u32[]{:S(2)}, u32[]{:S(2)}) collective-permute-start(bf16[512,128]{1,0:T(8,128)(2,1)S(1)} %get-tuple-element.178), channel_id=1, source_target_pairs={{0,2},{1,3},{2,0},{3,1},{4,6},{5,7},{6,4},{7,5},{8,10},{9,11},{10,... | collective-permute-start | bytes 393224 | tf_op jit(solution)/shard_map/ppermute | solution.py:706
  33.1 18.9 %collective-permute-start.3 = (bf16[512,512]{1,0:T(8,128)(2,1)S(1)}, bf16[512,512]{1,0:T(8,128)(2,1)S(1)}, u32[]{:S(2)}, u32[]{:S(2)}) collective-permute-start(bf16[512,512]{1,0:T(8,128)(2,1)S(1)} %get-tuple-element.59), channel_id=1, source_target_pairs={{0,1},{1,0},{2,3},{3,2},{4,5},{5,4},{6,7},{7,6},{8,9},{9,8},{10,11... | collective-permute-start | bytes 1572872 | tf_op jit(solution)/shard_map/ppermute | solution.py:706
  52.1 5.5 %collective-permute-start.7 = (bf16[512,128]{1,0:T(8,128)(2,1)S(1)}, bf16[512,128]{1,0:T(8,128)(2,1)S(1)}, u32[]{:S(2)}, u32[]{:S(2)}) collective-permute-start(bf16[512,128]{1,0:T(8,128)(2,1)S(1)} %get-tuple-element.177), channel_id=1, source_target_pairs={{0,3},{1,2},{2,1},{3,0},{4,7},{5,6},{6,5},{7,4},{8,11},{9,10},{10,... | collective-permute-start | bytes 393224 | tf_op jit(solution)/shard_map/ppermute | solution.py:706
  53.8 63.2 %collective-permute-start.21 = (bf16[1152,512]{1,0:T(8,128)(2,1)}, bf16[1152,512]{1,0:T(8,128)(2,1)}, u32[]{:S(2)}, u32[]{:S(2)}) collective-permute-start(bf16[1152,512]{1,0:T(8,128)(2,1)} %constant_dynamic-update-slice_fusion.3.w0), channel_id=1, source_target_pairs={{0,2},{1,3},{2,0},{3,1},{4,6},{5,7},{6,4},{7,5},{8,10},{9,11},{10,... | collective-permute-start | bytes 3538952 | tf_op jit(solution)/shard_map/ppermute | solution.py:706
  54.4 16.2 %collective-permute-start.2 = (bf16[512,512]{1,0:T(8,128)(2,1)S(1)}, bf16[512,512]{1,0:T(8,128)(2,1)S(1)}, u32[]{:S(2)}, u32[]{:S(2)}) collective-permute-start(bf16[512,512]{1,0:T(8,128)(2,1)S(1)} %get-tuple-element.57), channel_id=1, source_target_pairs={{0,1},{1,0},{2,3},{3,2},{4,5},{5,4},{6,7},{7,6},{8,9},{9,8},{10,11... | collective-permute-start | bytes 1572872 | tf_op jit(solution)/shard_map/ppermute | solution.py:706
  54.5 15.5 %collective-permute-start.10 = (bf16[128,512]{1,0:T(8,128)(2,1)S(1)}, bf16[128,512]{1,0:T(8,128)(2,1)S(1)}, u32[]{:S(2)}, u32[]{:S(2)}) collective-permute-start(bf16[128,512]{1,0:T(8,128)(2,1)S(1)} %collective-permute-done.9), channel_id=1, source_target_pairs={{0,1},{1,0},{2,3},{3,2},{4,5},{5,4},{6,7},{7,6},{8,9},{9,8},{10,11... | collective-permute-start | bytes 393224 | tf_op jit(solution)/shard_map/ppermute | solution.py:706
  57.5 37.5 %collective-permute-start.4 = (bf16[512,512]{1,0:T(8,128)(2,1)S(1)}, bf16[512,512]{1,0:T(8,128)(2,1)S(1)}, u32[]{:S(2)}, u32[]{:S(2)}) collective-permute-start(bf16[512,512]{1,0:T(8,128)(2,1)S(1)} %add_convert_fusion.1), channel_id=1, source_target_pairs={{0,2},{1,3},{2,0},{3,1},{4,6},{5,7},{6,4},{7,5},{8,10},{9,11},{10,... | collective-permute-start | bytes 1572872 | tf_op jit(solution)/shard_map/ppermute | solution.py:706
  69.0 72.5 %collective-permute-start.20 = (bf16[1152,512]{1,0:T(8,128)(2,1)}, bf16[1152,512]{1,0:T(8,128)(2,1)}, u32[]{:S(2)}, u32[]{:S(2)}) collective-permute-start(bf16[1152,512]{1,0:T(8,128)(2,1)} %constant_dynamic-update-slice_fusion.3.w0), channel_id=1, source_target_pairs={{0,1},{1,0},{2,3},{3,2},{4,5},{5,4},{6,7},{7,6},{8,9},{9,8},{10,11... | collective-permute-start | bytes 3538952 | tf_op jit(solution)/shard_map/ppermute | solution.py:706
  70.0 44.3 %collective-permute-start.15 = (bf16[3,128,512]{2,1,0:T(8,128)(2,1)S(1)}, bf16[3,128,512]{2,1,0:T(8,128)(2,1)}, u32[]{:S(2)}, u32[]{:S(2)}) collective-permute-start(bf16[3,128,512]{2,1,0:T(8,128)(2,1)S(1)} %bitcast.275), channel_id=1, source_target_pairs={{0,2},{1,3},{2,0},{3,1},{4,6},{5,7},{6,4},{7,5},{8,10},{9,11},{10,... | collective-permute-start | bytes 1179656 | tf_op jit(solution)/shard_map/ppermute | solution.py:706
  70.6 68.4 %collective-permute-start.17 = (bf16[512,128]{1,0:T(8,128)(2,1)}, bf16[512,128]{1,0:T(8,128)(2,1)}, u32[]{:S(2)}, u32[]{:S(2)}) collective-permute-start(bf16[512,128]{1,0:T(8,128)(2,1)} %get-tuple-element.172), channel_id=1, source_target_pairs={{0,1},{1,0},{2,3},{3,2},{4,5},{5,4},{6,7},{7,6},{8,9},{9,8},{10,11... | collective-permute-start | bytes 393224 | tf_op jit(solution)/shard_map/ppermute | solution.py:706
  114.3 25.0 %collective-permute-start.18 = (bf16[512,128]{1,0:T(8,128)(2,1)}, bf16[512,128]{1,0:T(8,128)(2,1)S(1)}, u32[]{:S(2)}, u32[]{:S(2)}) collective-permute-start(bf16[512,128]{1,0:T(8,128)(2,1)} %get-tuple-element.174), channel_id=1, source_target_pairs={{0,2},{1,3},{2,0},{3,1},{4,6},{5,7},{6,4},{7,5},{8,10},{9,11},{10,... | collective-permute-start | bytes 393224 | tf_op jit(solution)/shard_map/ppermute | solution.py:706
  117.0 22.3 %collective-permute-start.19 = (bf16[512,128]{1,0:T(8,128)(2,1)}, bf16[512,128]{1,0:T(8,128)(2,1)S(1)}, u32[]{:S(2)}, u32[]{:S(2)}) collective-permute-start(bf16[512,128]{1,0:T(8,128)(2,1)} %get-tuple-element.173), channel_id=1, source_target_pairs={{0,3},{1,2},{2,1},{3,0},{4,7},{5,6},{6,5},{7,4},{8,11},{9,10},{10,... | collective-permute-start | bytes 393224 | tf_op jit(solution)/shard_map/ppermute | solution.py:706
  117.4 24.1 %collective-permute-start.22 = (bf16[1152,512]{1,0:T(8,128)(2,1)}, bf16[1152,512]{1,0:T(8,128)(2,1)S(1)}, u32[]{:S(2)}, u32[]{:S(2)}) collective-permute-start(bf16[1152,512]{1,0:T(8,128)(2,1)} %collective-permute-done.21.w2), channel_id=1, source_target_pairs={{0,1},{1,0},{2,3},{3,2},{4,5},{5,4},{6,7},{7,6},{8,9},{9,8},{10,11... | collective-permute-start | bytes 3538952 | tf_op jit(solution)/shard_map/ppermute | solution.py:706
  163.3 176.0 %collective-permute-start.55 = (bf16[2,8,64,1152]{3,2,1,0:T(8,128)(2,1)}, bf16[2,8,64,1152]{3,2,1,0:T(8,128)(2,1)}, u32[]{:S(2)}, u32[]{:S(2)}) collective-permute-start(bf16[2,8,64,1152]{3,2,1,0:T(8,128)(2,1)} %second_weights.3), channel_id=1, source_target_pairs={{0,1},{1,0},{2,3},{3,2},{4,5},{5,4},{6,7},{7,6},{8,9},{9,8},{10,11... | collective-permute-start | bytes 7077896 | tf_op jit(solution)/shard_map/ppermute | solution.py:706
  163.6 9.0 %collective-permute-start.26 = (bf16[256,512]{1,0:T(8,128)(2,1)S(1)}, bf16[256,512]{1,0:T(8,128)(2,1)S(1)}, u32[]{:S(2)}, u32[]{:S(2)}) collective-permute-start(bf16[256,512]{1,0:T(8,128)(2,1)S(1)} %get-tuple-element.67), channel_id=1, source_target_pairs={{0,1},{1,0},{2,3},{3,2},{4,5},{5,4},{6,7},{7,6},{8,9},{9,8},{10,11... | collective-permute-start | bytes 786440 | tf_op jit(solution)/shard_map/ppermute | solution.py:706
  165.3 7.2 %collective-permute-start.24 = (bf16[512,128]{1,0:T(8,128)(2,1)S(1)}, bf16[512,128]{1,0:T(8,128)(2,1)S(1)}, u32[]{:S(2)}, u32[]{:S(2)}) collective-permute-start(bf16[512,128]{1,0:T(8,128)(2,1)S(1)} %get-tuple-element.170), channel_id=1, source_target_pairs={{0,2},{1,3},{2,0},{3,1},{4,6},{5,7},{6,4},{7,5},{8,10},{9,11},{10,... | collective-permute-start | bytes 393224 | tf_op jit(solution)/shard_map/ppermute | solution.py:706
  165.8 6.7 %collective-permute-start.25 = (bf16[512,128]{1,0:T(8,128)(2,1)S(1)}, bf16[512,128]{1,0:T(8,128)(2,1)S(1)}, u32[]{:S(2)}, u32[]{:S(2)}) collective-permute-start(bf16[512,128]{1,0:T(8,128)(2,1)S(1)} %get-tuple-element.169), channel_id=1, source_target_pairs={{0,1},{1,0},{2,3},{3,2},{4,5},{5,4},{6,7},{7,6},{8,9},{9,8},{10,11... | collective-permute-start | bytes 393224 | tf_op jit(solution)/shard_map/ppermute | solution.py:706
  225.4 36.2 %collective-permute-start.31 = (bf16[512,512]{1,0:T(8,128)(2,1)S(1)}, bf16[512,512]{1,0:T(8,128)(2,1)S(1)}, u32[]{:S(2)}, u32[]{:S(2)}) collective-permute-start(bf16[512,512]{1,0:T(8,128)(2,1)S(1)} %get-tuple-element.76.grads.refs_4_), channel_id=1, source_target_pairs={{0,2},{1,3},{2,0},{3,1},{4,6},{5,7},{6,4},{7,5},{8,10},{9,11},{10,... | collective-permute-start | bytes 1572872 | tf_op jit(solution)/shard_map/ppermute | solution.py:706
  245.7 9.3 %collective-permute-start.50 = (bf16[2,8,64,128]{3,2,1,0:T(8,128)(2,1)}, bf16[2,8,64,128]{3,2,1,0:T(8,128)(2,1)S(1)}, u32[]{:S(2)}, u32[]{:S(2)}) collective-permute-start(bf16[2,8,64,128]{3,2,1,0:T(8,128)(2,1)} %pad_maximum_fusion.7), channel_id=1, source_target_pairs={{0,1},{1,0},{2,3},{3,2},{4,5},{5,4},{6,7},{7,6},{8,9},{9,8},{10,11... | collective-permute-start | bytes 786440 | tf_op jit(solution)/shard_map/ppermute | solution.py:706
  250.4 7.2 %collective-permute-start.28 = (bf16[512,128]{1,0:T(8,128)(2,1)}, bf16[512,128]{1,0:T(8,128)(2,1)}, u32[]{:S(2)}, u32[]{:S(2)}) collective-permute-start(bf16[512,128]{1,0:T(8,128)(2,1)} %get-tuple-element.168), channel_id=1, source_target_pairs={{0,3},{1,2},{2,1},{3,0},{4,7},{5,6},{6,5},{7,4},{8,11},{9,10},{10,... | collective-permute-start | bytes 393224 | tf_op jit(solution)/shard_map/ppermute | solution.py:706
  251.8 7.4 %collective-permute-start.29 = (bf16[512,128]{1,0:T(8,128)(2,1)}, bf16[512,128]{1,0:T(8,128)(2,1)S(1)}, u32[]{:S(2)}, u32[]{:S(2)}) collective-permute-start(bf16[512,128]{1,0:T(8,128)(2,1)} %get-tuple-element.167), channel_id=1, source_target_pairs={{0,2},{1,3},{2,0},{3,1},{4,6},{5,7},{6,4},{7,5},{8,10},{9,11},{10,... | collective-permute-start | bytes 393224 | tf_op jit(solution)/shard_map/ppermute | solution.py:706
  257.7 19.1 %collective-permute-start.33 = (bf16[512,512]{1,0:T(8,128)(2,1)S(1)}, bf16[512,512]{1,0:T(8,128)(2,1)S(1)}, u32[]{:S(2)}, u32[]{:S(2)}) collective-permute-start(bf16[512,512]{1,0:T(8,128)(2,1)S(1)} %get-tuple-element.76.grads.refs_4_), channel_id=1, source_target_pairs={{0,1},{1,0},{2,3},{3,2},{4,5},{5,4},{6,7},{7,6},{8,9},{9,8},{10,11... | collective-permute-start | bytes 1572872 | tf_op jit(solution)/shard_map/ppermute | solution.py:706
  259.2 14.2 %collective-permute-start.51 = (bf16[8,64,512]{2,1,0:T(8,128)(2,1)}, bf16[8,64,512]{2,1,0:T(8,128)(2,1)}, u32[]{:S(2)}, u32[]{:S(2)}) collective-permute-start(bf16[8,64,512]{2,1,0:T(8,128)(2,1)} %fusion.15), channel_id=1, source_target_pairs={{0,2},{1,3},{2,0},{3,1},{4,6},{5,7},{6,4},{7,5},{8,10},{9,11},{10,... | collective-permute-start | bytes 1572872 | tf_op jit(solution)/shard_map/ppermute | solution.py:706
  271.4 17.0 %collective-permute-start.32 = (bf16[512,512]{1,0:T(8,128)(2,1)S(1)}, bf16[512,512]{1,0:T(8,128)(2,1)S(1)}, u32[]{:S(2)}, u32[]{:S(2)}) collective-permute-start(bf16[512,512]{1,0:T(8,128)(2,1)S(1)} %collective-permute-done.31.grads.refs_6_), channel_id=1, source_target_pairs={{0,1},{1,0},{2,3},{3,2},{4,5},{5,4},{6,7},{7,6},{8,9},{9,8},{10,11... | collective-permute-start | bytes 1572872 | tf_op jit(solution)/shard_map/ppermute | solution.py:706
  274.7 11.9 %collective-permute-start.52 = (bf16[4,64,512]{2,1,0:T(8,128)(2,1)S(1)}, bf16[4,64,512]{2,1,0:T(8,128)(2,1)}, u32[]{:S(2)}, u32[]{:S(2)}) collective-permute-start(bf16[4,64,512]{2,1,0:T(8,128)(2,1)S(1)} %dynamic-slice_bitcast_fusion.8), channel_id=1, source_target_pairs={{0,4},{4,0},{8,12},{12,8},{16,20},{20,16},{24,28},{28,24},{1,5},{5... | collective-permute-start | bytes 786440 | tf_op jit(solution)/shard_map/ppermute | solution.py:706
  288.3 37.1 %collective-permute-start.53 = (bf16[2,64,512]{2,1,0:T(8,128)(2,1)}, bf16[2,64,512]{2,1,0:T(8,128)(2,1)}, u32[]{:S(2)}, u32[]{:S(2)}) collective-permute-start(bf16[2,64,512]{2,1,0:T(8,128)(2,1)} %dynamic-slice_bitcast_fusion.9), channel_id=1, source_target_pairs={{0,8},{4,12},{8,0},{12,4},{16,24},{20,28},{24,16},{28,20},{1,9},{5... | collective-permute-start | bytes 393224 | tf_op jit(solution)/shard_map/ppermute | solution.py:706
  295.5 47.4 %collective-permute-start.36 = (bf16[4,64,1152]{2,1,0:T(8,128)(2,1)}, bf16[4,64,1152]{2,1,0:T(8,128)(2,1)}, u32[]{:S(2)}, u32[]{:S(2)}) collective-permute-start(bf16[4,64,1152]{2,1,0:T(8,128)(2,1)} %dynamic-slice_bitcast_fusion.3), channel_id=1, source_target_pairs={{0,4},{4,0},{8,12},{12,8},{16,20},{20,16},{24,28},{28,24},{1,5},{5... | collective-permute-start | bytes 1769480 | tf_op jit(solution)/shard_map/ppermute | solution.py:706
  303.8 40.9 %collective-permute-start.39 = (bf16[4,64,1152]{2,1,0:T(8,128)(2,1)}, bf16[4,64,1152]{2,1,0:T(8,128)(2,1)}, u32[]{:S(2)}, u32[]{:S(2)}) collective-permute-start(bf16[4,64,1152]{2,1,0:T(8,128)(2,1)} %dynamic-slice_bitcast_fusion.2), channel_id=1, source_target_pairs={{0,4},{4,0},{8,12},{12,8},{16,20},{20,16},{24,28},{28,24},{1,5},{5... | collective-permute-start | bytes 1769480 | tf_op jit(solution)/shard_map/ppermute | solution.py:706
  316.2 11.6 %collective-permute-start.34 = (bf16[128,256]{0,1:T(8,128)(2,1)S(1)}, bf16[128,256]{0,1:T(8,128)(2,1)S(1)}, u32[]{:S(2)}, u32[]{:S(2)}) collective-permute-start(bf16[128,256]{0,1:T(8,128)(2,1)S(1)} %get-tuple-element.155), channel_id=1, source_target_pairs={{0,4},{4,8},{8,12},{12,16},{16,20},{20,24},{24,28},{1,5},{5,9},{9,... | collective-permute-start | bytes 196616 | tf_op jit(solution)/shard_map/ppermute | solution.py:903
  325.4 7.3 %collective-permute-start.35 = (bf16[128,256]{0,1:T(8,128)(2,1)S(1)}, bf16[128,256]{0,1:T(8,128)(2,1)S(1)}, u32[]{:S(2)}, u32[]{:S(2)}) collective-permute-start(bf16[128,256]{0,1:T(8,128)(2,1)S(1)} %get-tuple-element.156), channel_id=1, source_target_pairs={{4,0},{8,4},{12,8},{16,12},{20,16},{24,20},{28,24},{5,1},{9,5},{13... | collective-permute-start | bytes 196616 | tf_op jit(solution)/shard_map/ppermute | solution.py:902
  327.8 19.8 %collective-permute-start.42 = (bf16[4,64,1152]{2,1,0:T(8,128)(2,1)S(1)}, bf16[4,64,1152]{2,1,0:T(8,128)(2,1)S(1)}, u32[]{:S(2)}, u32[]{:S(2)}) collective-permute-start(bf16[4,64,1152]{2,1,0:T(8,128)(2,1)S(1)} %dynamic-slice_bitcast_fusion.1), channel_id=1, source_target_pairs={{0,4},{4,0},{8,12},{12,8},{16,20},{20,16},{24,28},{28,24},{1,5},{5... | collective-permute-start | bytes 1769480 | tf_op jit(solution)/shard_map/ppermute | solution.py:706
  341.7 24.3 %collective-permute-start.56 = (bf16[8,64,1152]{2,1,0:T(8,128)(2,1)S(1)}, bf16[8,64,1152]{2,1,0:T(8,128)(2,1)S(1)}, u32[]{:S(2)}, u32[]{:S(2)}) collective-permute-start(bf16[8,64,1152]{2,1,0:T(8,128)(2,1)S(1)} %slice_bitcast_fusion), channel_id=1, source_target_pairs={{0,2},{1,3},{2,0},{3,1},{4,6},{5,7},{6,4},{7,5},{8,10},{9,11},{10,... | collective-permute-start | bytes 3538952 | tf_op jit(solution)/shard_map/ppermute | solution.py:706
  344.2 13.2 %collective-permute-start.37 = (bf16[2,64,1152]{2,1,0:T(8,128)(2,1)S(1)}, bf16[2,64,1152]{2,1,0:T(8,128)(2,1)S(1)}, u32[]{:S(2)}, u32[]{:S(2)}) collective-permute-start(bf16[2,64,1152]{2,1,0:T(8,128)(2,1)S(1)} %dynamic-slice_bitcast_fusion.7), channel_id=1, source_target_pairs={{0,8},{4,12},{8,0},{12,4},{16,24},{20,28},{24,16},{28,20},{1,9},{5... | collective-permute-start | bytes 884744 | tf_op jit(solution)/shard_map/ppermute | solution.py:706
  346.0 15.1 %collective-permute-start.40 = (bf16[2,64,1152]{2,1,0:T(8,128)(2,1)S(1)}, bf16[2,64,1152]{2,1,0:T(8,128)(2,1)S(1)}, u32[]{:S(2)}, u32[]{:S(2)}) collective-permute-start(bf16[2,64,1152]{2,1,0:T(8,128)(2,1)S(1)} %dynamic-slice_bitcast_fusion.6), channel_id=1, source_target_pairs={{0,8},{4,12},{8,0},{12,4},{16,24},{20,28},{24,16},{28,20},{1,9},{5... | collective-permute-start | bytes 884744 | tf_op jit(solution)/shard_map/ppermute | solution.py:706
  347.9 17.9 %collective-permute-start.43 = (bf16[2,64,1152]{2,1,0:T(8,128)(2,1)S(1)}, bf16[2,64,1152]{2,1,0:T(8,128)(2,1)S(1)}, u32[]{:S(2)}, u32[]{:S(2)}) collective-permute-start(bf16[2,64,1152]{2,1,0:T(8,128)(2,1)S(1)} %dynamic-slice_bitcast_fusion.5), channel_id=1, source_target_pairs={{0,8},{4,12},{8,0},{12,4},{16,24},{20,28},{24,16},{28,20},{1,9},{5... | collective-permute-start | bytes 884744 | tf_op jit(solution)/shard_map/ppermute | solution.py:706
  357.5 12.1 %collective-permute-start.38 = (bf16[1,64,1152]{2,1,0:T(8,128)(2,1)S(1)}, bf16[1,64,1152]{2,1,0:T(8,128)(2,1)S(1)}, u32[]{:S(2)}, u32[]{:S(2)}) collective-permute-start(bf16[1,64,1152]{2,1,0:T(8,128)(2,1)S(1)} %constant_dynamic-slice_fusion.4), channel_id=1, source_target_pairs={{0,16},{4,20},{8,24},{12,28},{16,0},{20,4},{24,8},{28,12},{1,17},{... | collective-permute-start | bytes 442376 | tf_op jit(solution)/shard_map/ppermute | solution.py:706
  361.1 16.2 %collective-permute-start.41 = (bf16[1,64,1152]{2,1,0:T(8,128)(2,1)S(1)}, bf16[1,64,1152]{2,1,0:T(8,128)(2,1)S(1)}, u32[]{:S(2)}, u32[]{:S(2)}) collective-permute-start(bf16[1,64,1152]{2,1,0:T(8,128)(2,1)S(1)} %constant_dynamic-slice_fusion.3), channel_id=1, source_target_pairs={{0,16},{4,20},{8,24},{12,28},{16,0},{20,4},{24,8},{28,12},{1,17},{... | collective-permute-start | bytes 442376 | tf_op jit(solution)/shard_map/ppermute | solution.py:706
  366.3 10.7 %collective-permute-start.57 = (bf16[4,64,1152]{2,1,0:T(8,128)(2,1)S(1)}, bf16[4,64,1152]{2,1,0:T(8,128)(2,1)S(1)}, u32[]{:S(2)}, u32[]{:S(2)}) collective-permute-start(bf16[4,64,1152]{2,1,0:T(8,128)(2,1)S(1)} %dynamic-slice_bitcast_fusion), channel_id=1, source_target_pairs={{0,4},{4,0},{8,12},{12,8},{16,20},{20,16},{24,28},{28,24},{1,5},{5... | collective-permute-start | bytes 1769480 | tf_op jit(solution)/shard_map/ppermute | solution.py:706
  368.6 17.9 %collective-permute-start.44 = (bf16[1,64,1152]{2,1,0:T(8,128)(2,1)S(1)}, bf16[1,64,1152]{2,1,0:T(8,128)(2,1)S(1)}, u32[]{:S(2)}, u32[]{:S(2)}) collective-permute-start(bf16[1,64,1152]{2,1,0:T(8,128)(2,1)S(1)} %constant_dynamic-slice_fusion.2), channel_id=1, source_target_pairs={{0,16},{4,20},{8,24},{12,28},{16,0},{20,4},{24,8},{28,12},{1,17},{... | collective-permute-start | bytes 442376 | tf_op jit(solution)/shard_map/ppermute | solution.py:706
  377.3 8.4 %collective-permute-start.58 = (bf16[2,64,1152]{2,1,0:T(8,128)(2,1)S(1)}, bf16[2,64,1152]{2,1,0:T(8,128)(2,1)S(1)}, u32[]{:S(2)}, u32[]{:S(2)}) collective-permute-start(bf16[2,64,1152]{2,1,0:T(8,128)(2,1)S(1)} %dynamic-slice_bitcast_fusion.4), channel_id=1, source_target_pairs={{0,8},{4,12},{8,0},{12,4},{16,24},{20,28},{24,16},{28,20},{1,9},{5... | collective-permute-start | bytes 884744 | tf_op jit(solution)/shard_map/ppermute | solution.py:706
  385.7 7.1 %collective-permute-start.59 = (bf16[1,64,1152]{2,1,0:T(8,128)(2,1)S(1)}, bf16[1,64,1152]{2,1,0:T(8,128)(2,1)S(1)}, u32[]{:S(2)}, u32[]{:S(2)}) collective-permute-start(bf16[1,64,1152]{2,1,0:T(8,128)(2,1)S(1)} %constant_dynamic-slice_fusion), channel_id=1, source_target_pairs={{0,16},{4,20},{8,24},{12,28},{16,0},{20,4},{24,8},{28,12},{1,17},{... | collective-permute-start | bytes 442376 | tf_op jit(solution)/shard_map/ppermute | solution.py:706
  (77 other events, 479.1 us)
